TPU v7x, 128 devices: a whole 4x4x4 slice. The times are simulated.
128 devices in a mesh: gx: 4 (over y_hi, core), gy: 4 (over x), gz: 8 (over z, y_lo).
Axes of the slice: x: 4, y: 4 (y_hi: 2, y_lo: 2; y = y_hi * 2 + y_lo), z: 4, core: 2. Of those that a mesh axis runs over, the one named last changes fastest.
Arguments:
- vol_field: float32 [8, 128, 64, 1024], P(None, 'gx', 'gy', 'gz'), may hold values from -6 to 6
- scaling: float32 [128, 64, 1024], P('gx', 'gy', 'gz'), may hold values from 0.5 to 2
- diag_shift: float32 [128, 64, 1024], P('gx', 'gy', 'gz'), may hold values from 0.5 to 2
- bnd_field: float32 [8, 16384], P(None, ('gx', 'gy', 'gz')), may hold values from -6 to 6
- bnd_cell: int32 [16384], P(('gx', 'gy', 'gz')), may hold values from 0 to 65535, as said below
- labels: int32 [16384], P(('gx', 'gy', 'gz')), may hold values from 0 to 31
- lr_left: bfloat16 [64, 64, 32, 256], P(('gx', 'gy'), 'gz'), may hold values from -1 to 1
- lr_right: bfloat16 [64, 64, 32, 256], P(('gx', 'gy'), 'gz'), may hold values from -0.046875 to 0.046875
- near_tiles: bfloat16 [64, 8, 256, 256], P(('gx', 'gy'), 'gz'), may hold values from -0.125 to 0.125
- near_slot: int32 [64, 64], P(('gx', 'gy'), 'gz'), may hold values from -1 to 0, as said below
Outputs:
- vol_out: float32 [8, 128, 64, 1024], P(None, 'gx', 'gy', 'gz')
- bnd_out: float32 [8, 16384], P(None, ('gx', 'gy', 'gz'))
- charges: float32 [32, 8], replicated
Inputs may be any that keep to these rules, and one draw needn't show every extreme that they name: `bnd_cell`: within each block of 128 entries owned by one device the cells are distinct. `near_slot`: each tile row holds, within each column group of 8 tiles, exactly one near-field tile (slot 0); all other entries are -1, and the factors of near-field tiles are not used.
All inputs are finite; a program needn't handle non-finite values.
Results may differ from a plain program's by a relative error of at most 0.0003.
Values sent between devices are 32-bit elements; how exact they have to be, the bound alone decides.
A program may use at most 128 MiB of HBM per device.

v0:
```python
import jax
import jax.numpy as jnp
from jax import lax
from jax.sharding import PartitionSpec as P

CONDUCTORS = 32


HIGHEST = lax.Precision.HIGHEST


def extended(array, sides, width):
    for axis, dim in sides:
        devices, length = (lax.axis_size(axis), array.shape[dim])
        up = [(i, (i + 1) % devices) for i in range(devices - 1)]
        down = [(j, i) for i, j in up]
        last = lax.slice_in_dim(array, length - width, length, axis=dim)
        initial = lax.slice_in_dim(array, 0, width, axis=dim)
        before = lax.ppermute(last, axis, up)
        after = lax.ppermute(initial, axis, down)
        array = jnp.concatenate([before, array, after], axis=dim)
    return array


def apply_line(values, axis_dim, use_mass):
    length = values.shape[axis_dim]
    lower_cells = lax.slice_in_dim(values, 0, length - 2, axis=axis_dim)
    middle = lax.slice_in_dim(values, 1, length - 1, axis=axis_dim)
    upper_cells = lax.slice_in_dim(values, 2, length, axis=axis_dim)
    if use_mass:
        return (lower_cells + 4.0 * middle + upper_cells) / 6.0
    return 2.0 * middle - lower_cells - upper_cells


def stiffness(scaled):
    padded = extended(scaled, (("gx", 1), ("gy", 2), ("gz", 3)), 1)
    mass_x = apply_line(padded, 1, True)
    stiff_x = apply_line(padded, 1, False)
    mass_xy = apply_line(mass_x, 2, True)
    stiff_xy = apply_line(mass_x, 2, False) + apply_line(stiff_x, 2, True)
    return apply_line(stiff_xy, 3, True) + apply_line(mass_xy, 3, False)


def shards(
    vol_field,
    scaling,
    diag_shift,
    bnd_field,
    bnd_cell,
    labels,
    lr_left,
    lr_right,
    near_tiles,
    near_slot,
):
    columns, size_x, size_y, size_z = vol_field.shape
    vol_base = scaling * stiffness(scaling * vol_field) + diag_shift * vol_field
    traced_vol = jnp.take(vol_field.reshape(columns, size_x * size_y * size_z), bnd_cell, axis=1)
    vol_out = (
        vol_base.reshape(columns, size_x * size_y * size_z)
        .at[:, bnd_cell]
        .add(bnd_field)
        .reshape(vol_field.shape)
    )
    col_index = lax.axis_index("gz")
    group_count = lax.axis_size("gz")
    gathered = lax.all_gather(bnd_field, ("gx", "gy", "gz"), axis=1, tiled=True)
    col_width = gathered.shape[1] // group_count
    x_column = lax.dynamic_slice_in_dim(gathered, col_index * col_width, col_width, 1)
    row_tiles, col_tiles, rank_size, tile_size = lr_left.shape
    slot_count = near_tiles.shape[1]
    x_tiles = x_column.reshape(columns, col_tiles, tile_size)
    far_mask = (near_slot < 0).astype(jnp.float32)
    projected = jnp.einsum(
        "ijrt,cjt->ijrc", lr_right.astype(jnp.float32), x_tiles, precision=HIGHEST
    )
    projected = projected * far_mask[:, :, None, None]
    far_field = jnp.einsum(
        "ijrt,ijrc->cit", lr_left.astype(jnp.float32), projected, precision=HIGHEST
    )
    picked = (
        near_slot[:, :, None] == jnp.arange(slot_count, dtype=jnp.int32)[None, None, :]
    ).astype(jnp.float32)
    chosen = jnp.einsum("ijs,cju->iscu", picked, x_tiles, precision=HIGHEST)
    near_field = jnp.einsum(
        "istu,iscu->cit", near_tiles.astype(jnp.float32), chosen, precision=HIGHEST
    )
    partial_value = (far_field + near_field).reshape(columns, row_tiles * tile_size)
    summed = lax.psum(partial_value, "gz")
    share_width = summed.shape[1] // group_count
    row_share = lax.dynamic_slice_in_dim(summed, col_index * share_width, share_width, 1)
    bnd_out = traced_vol - row_share
    member = (labels[None, :] == jnp.arange(CONDUCTORS, dtype=jnp.int32)[:, None]).astype(
        jnp.float32
    )
    local_sum = jnp.dot(member, bnd_out.T, precision=HIGHEST)
    total_nodes = row_tiles * tile_size * lax.axis_size(("gx", "gy"))
    charges = lax.psum(local_sum, ("gx", "gy", "gz")) * (CONDUCTORS / total_nodes) ** 0.5
    return (vol_out, bnd_out, charges)


def solution(mesh):
    in_specs = (
        P(None, "gx", "gy", "gz"),
        P("gx", "gy", "gz"),
        P("gx", "gy", "gz"),
        P(None, ("gx", "gy", "gz")),
        P(("gx", "gy", "gz")),
        P(("gx", "gy", "gz")),
        P(("gx", "gy"), "gz", None, None),
        P(("gx", "gy"), "gz", None, None),
        P(("gx", "gy"), "gz", None, None),
        P(("gx", "gy"), "gz"),
    )
    out_specs = (P(None, "gx", "gy", "gz"), P(None, ("gx", "gy", "gz")), P())
    return jax.shard_map(shards, mesh=mesh, in_specs=in_specs, out_specs=out_specs, check_vma=False)
```

profile of v0, /device:TPU:1, one launch (start us, length us, event | category | flops | bytes accessed | tf_op | source)
XLA Modules:
  0.0 560.4 jit_solution(10669513463929413623)
XLA Ops:
  0.6 0.0 copy-start
  0.6 2.9 copy_multiply_fusion
  3.5 6.2 %collective-permute-start = (f32[8,1,16,128]{3,0,2,1:T(8,128)S(1)}, f32[8,1,16,128]{3,0,2,1:T(8,128)S(1)}, u32[]{:S(2)}, u32[]{:S(2)}) collective-permute-start(f32[8,1,16,128]{3,0,2,1:T(8,128)S(1)} %get-tuple-element.20), channel_id=1, source_target_pairs={{0,32},{32,64},{64,96},{1,33},{33,65},{65,97},{2,34},{34,66},{66,9... | collective-permute-start | bytes 196616 | tf_op jit(solution)/shard_map/ppermute | solution.py:19
  9.8 1.9 collective-permute-start.1
  11.7 0.0 copy-start.8
  11.7 0.0 copy-start.5
  11.7 0.0 copy-start.6
  11.7 17.5 %copy.32 = f32[8,32,16,128]{0,3,2,1:T(8,128)} copy(f32[8,32,16,128]{3,2,1,0:T(8,128)} %param.10) | data formatting | bytes 4194304 | tf_op args[0]
  29.3 278.9 %all_gather.3 = f32[8,16384]{1,0:T(8,128)S(1)} all-gather(f32[8,128]{1,0:T(8,128)S(1)} %copy-done.5), channel_id=1, replica_groups=mesh['gx'=4,'gy'=4,'gz'=8] {'gx','gy','gz'}, dimensions={1}, use_global_device_ids=true | all-gather | bytes 528384 | tf_op jit(solution)/shard_map/all_gather | solution.py:67
  308.2 0.2 fusion.12
  308.4 0.5 fusion.10
  308.9 2.2 fusion.8
  311.1 1.5 fusion.9
  312.6 0.2 copy.35
  312.8 32.6 %psum.14 = f32[8,1024]{0,1:T(8,128)S(1)} all-reduce(f32[8,1024]{0,1:T(8,128)S(1)} %copy.35), channel_id=1, replica_groups=mesh['gx'=4,'gy'=4,'gz'=8] {'gz'}, use_global_device_ids=true, to_apply=%region_1.2 | all-reduce | flops 8192 | bytes 65536 | tf_op jit(solution)/shard_map/psum | solution.py:89
  345.5 11.2 %gather_fusion = f32[128,8]{1,0:T(8,128)S(1)} fusion(f32[8,65536]{0,1:T(8,128)} %bitcast.34, s32[1024]{0:T(1024)S(1)} %pad_clamp_fusion), kind=kCustom, calls=%fused_computation | custom fusion | bytes 8704 | tf_op jit(solution)/shard_map/jit(_take)/gather | solution.py:58
  356.7 0.1 bitcast_subtract_fusion
  356.8 0.0 collective-permute-done
  356.8 0.0 collective-permute-done.1
  356.8 1.3 collective-permute-start.2
  358.1 1.3 collective-permute-start.3
  359.5 0.2 fusion.15
  359.6 108.0 %psum.15 = f32[32,8]{0,1:T(8,128)S(1)} all-reduce(f32[32,8]{0,1:T(8,128)S(1)} %fusion.15), channel_id=1, replica_groups=mesh['gx'=4,'gy'=4,'gz'=8] {'gx','gy','gz'}, use_global_device_ids=true, to_apply=%region_2.3 | all-reduce | flops 256 | bytes 2048 | tf_op jit(solution)/shard_map/psum | solution.py:98
  467.7 0.0 collective-permute-done.2
  467.7 0.0 collective-permute-done.3
  467.7 0.2 pad_maximum_fusion.1
  467.9 3.0 fusion.21
  470.9 2.9 copy.25
  473.7 2.8 collective-permute-start.4
  476.6 2.9 copy.26
  479.4 1.5 collective-permute-start.5
  480.9 0.6 broadcast_multiply_fusion
  481.5 0.7 copy.37
  482.2 0.1 copy.31
  482.3 0.0 collective-permute-done.4
  482.3 2.6 copy.27
  484.9 0.0 collective-permute-done.5
  484.9 2.6 copy.28
  487.5 6.1 %pad_maximum_fusion = f32[8,34,18,130]{3,0,2,1:T(8,128)S(1)} fusion(f32[8,34,18,1]{3,0,2,1:T(8,128)} %copy.28, f32[8,34,1,128]{3,0,2,1:T(8,128)S(1)} %collective-permute-done.3, f32[8,1,16,128]{3,0,2,1:T(8,128)S(1)} %collective-permute-done.1, f32[8,32,16,128]{3,0,2,1:T(8,128)S(1)} %copy_multiply_fusion, f32[8,1,16,128]{3,0,2,1:T(8,128)S(1)} %collective-permute-done, ...), kind=kLoop, calls=%fused_computation.2 | loop fusion | flops 3818880 | bytes 5091840 | tf_op jit(solution)/shard_map/concatenate | solution.py:21
  493.6 1.3 subtract_subtract_fusion
  494.9 0.0 copy-start.2
  494.9 0.0 copy-start.3
  494.9 0.0 copy-start.4
  494.9 2.9 fusion.1
  497.9 4.1 fusion.5
  502.0 16.2 %copy.30 = f32[8,32,16,128]{0,3,2,1:T(8,128)} copy(f32[8,32,16,128]{3,0,2,1:T(8,128)} %fusion.5) | data formatting | bytes 4194304 | tf_op jit(solution)/shard_map/add | solution.py:57
  518.2 22.7 %scatter_fusion = f32[8,65536]{0,1:T(8,128)} fusion(f32[8,65536]{0,1:T(8,128)} %bitcast.32, s32[128]{0:T(128)S(1)} %compare_select_fusion, f32[128,8]{1,0:T(8,128)S(1)} %copy.31), kind=kCustom, calls=%fused_computation.1 | custom fusion | flops 1024 | bytes 12800 | tf_op jit(solution)/shard_map/scatter-add | solution.py:62
  541.0 19.5 %copy.36 = f32[8,32,16,128]{3,2,1,0:T(8,128)} copy(f32[8,32,16,128]{0,3,2,1:T(8,128)} %bitcast.33) | data formatting | bytes 4194304
  (18 shorter events, 0.1 us)
Async XLA Ops:
  0.6 307.8 %copy-start = (bf16[4,1,256,256]{3,2,1,0:T(8,128)(2,1)S(1)}, bf16[4,1,256,256]{3,2,1,0:T(8,128)(2,1)}, u32[]{:S(2)}) copy-start(bf16[4,1,256,256]{3,2,1,0:T(8,128)(2,1)} %param.18) | copy-start | bytes 1572868
  3.5 353.3 %collective-permute-start = (f32[8,1,16,128]{3,0,2,1:T(8,128)S(1)}, f32[8,1,16,128]{3,0,2,1:T(8,128)S(1)}, u32[]{:S(2)}, u32[]{:S(2)}) collective-permute-start(f32[8,1,16,128]{3,0,2,1:T(8,128)S(1)} %get-tuple-element.20), channel_id=1, source_target_pairs={{0,32},{32,64},{64,96},{1,33},{33,65},{65,97},{2,34},{34,66},{66,9... | collective-permute-start | bytes 196616 | tf_op jit(solution)/shard_map/ppermute | solution.py:19
  9.8 347.0 %collective-permute-start.1 = (f32[8,1,16,128]{3,0,2,1:T(8,128)S(1)}, f32[8,1,16,128]{3,0,2,1:T(8,128)S(1)}, u32[]{:S(2)}, u32[]{:S(2)}) collective-permute-start(f32[8,1,16,128]{3,0,2,1:T(8,128)S(1)} %get-tuple-element.21), channel_id=1, source_target_pairs={{32,0},{64,32},{96,64},{33,1},{65,33},{97,65},{34,2},{66,34},{98,6... | collective-permute-start | bytes 196616 | tf_op jit(solution)/shard_map/ppermute | solution.py:20
  11.7 17.6 %copy-start.8 = (s32[128]{0:T(128)S(1)}, s32[128]{0:T(128)}, u32[]{:S(2)}) copy-start(s32[128]{0:T(128)} %param.14) | copy-start | bytes 1540
  11.7 17.6 %copy-start.5 = (f32[8,128]{1,0:T(8,128)S(1)}, f32[8,128]{1,0:T(8,128)}, u32[]{:S(2)}) copy-start(f32[8,128]{1,0:T(8,128)} %param.13) | copy-start | bytes 12292
  11.7 296.5 %copy-start.6 = (s32[4,8]{1,0:T(4,128)S(1)}, s32[4,8]{1,0:T(4,128)}, u32[]{:S(2)}) copy-start(s32[4,8]{1,0:T(4,128)} %param.19) | copy-start | bytes 388
  29.2 330.2 %copy-start.7 = (s32[128]{0:T(128)S(1)}, s32[128]{0:T(128)}, u32[]{:S(2)}) copy-start(s32[128]{0:T(128)} %param.15) | copy-start | bytes 1540
  356.8 110.8 %collective-permute-start.2 = (f32[8,34,1,128]{3,0,2,1:T(8,128)S(1)}, f32[8,34,1,128]{3,0,2,1:T(8,128)S(1)}, u32[]{:S(2)}, u32[]{:S(2)}) collective-permute-start(f32[8,34,1,128]{3,0,2,1:T(8,128)S(1)} %get-tuple-element.18), channel_id=1, source_target_pairs={{0,8},{8,16},{16,24},{1,9},{9,17},{17,25},{2,10},{10,18},{18,26},{... | collective-permute-start | bytes 417800 | tf_op jit(solution)/shard_map/ppermute | solution.py:19
  358.1 109.5 %collective-permute-start.3 = (f32[8,34,1,128]{3,0,2,1:T(8,128)S(1)}, f32[8,34,1,128]{3,0,2,1:T(8,128)S(1)}, u32[]{:S(2)}, u32[]{:S(2)}) collective-permute-start(f32[8,34,1,128]{3,0,2,1:T(8,128)S(1)} %get-tuple-element.19), channel_id=1, source_target_pairs={{8,0},{16,8},{24,16},{9,1},{17,9},{25,17},{10,2},{18,10},{26,18},{... | collective-permute-start | bytes 417800 | tf_op jit(solution)/shard_map/ppermute | solution.py:20
  473.7 8.5 %collective-permute-start.4 = (f32[8,34,18,1]{1,0,3,2:T(8,128)S(1)}, f32[8,34,18,1]{1,0,3,2:T(8,128)S(1)}, u32[]{:S(2)}, u32[]{:S(2)}) collective-permute-start(f32[8,34,18,1]{1,0,3,2:T(8,128)S(1)} %copy.25), channel_id=1, source_target_pairs={{0,1},{1,2},{2,3},{3,4},{4,5},{5,6},{6,7},{8,9},{9,10},{10,11},{11... | collective-permute-start | bytes 58760 | tf_op jit(solution)/shard_map/ppermute | solution.py:19
  479.4 5.5 collective-permute-start.5
  494.9 2.9 copy-start.2
  494.9 2.9 copy-start.3
  494.9 2.9 copy-start.4
  541.0 19.5 %copy-start.1 = (bf16[4,1,256,256]{3,2,1,0:T(8,128)(2,1)S(1)}, bf16[4,1,256,256]{3,2,1,0:T(8,128)(2,1)}, u32[]{:S(2)}) copy-start(bf16[4,1,256,256]{3,2,1,0:T(8,128)(2,1)} %param.18) | copy-start | bytes 1572868
where the time goes:
time: 563 us; the launch traced here: 560 us
  blocking collectives  420 us (75%)
  local copies, waits for them, and re-layouts  79.4 us (14%)
  other arithmetic  40.9 us (7%)
  starting transfers between devices  15 us (3%)
    all_gather x1, blocking collectives, shards(): gathered = lax.all_gather(bnd_field, ('gx', 'gy', 'gz'), axis=1, tiled=True)  279 us
    psum x1, blocking collectives, shards(): lax.psum(local_sum, ('gx', 'gy', 'gz')) * (CONDUCTORS / total_nodes) ** 0.5  108 us
    unnamed x22, local copies, waits for them, and re-layouts  37.8 us
    psum x1, blocking collectives, shards(): summed = lax.psum(partial_value, 'gz')  32.6 us
    scatter-add x1, other arithmetic, shards(): vol_out = vol_base.reshape(columns, size_x * size_y * size_z).at[:, bnd_c...  22.7 us
    add x1, local copies, waits for them, and re-layouts, shards(): vol_base = scaling * stiffness(scaling * vol_field) + diag_shift * vol_field  16.2 us
  transfers between devices with their start and end apart: 6, of which 0 were waited for; matrix products, arithmetic and copies ran while one was open for 7% of the time, Pallas kernels for 0%

commit v1 on v0

v1 whole, which is shorter than its diff:
```python
import functools

import jax
import jax.numpy as jnp
from jax import lax
from jax.experimental import pallas as pl
from jax.experimental.pallas import tpu as pltpu
from jax.sharding import PartitionSpec as P

MESH = pl.DeviceIdType.MESH
F32 = jnp.float32
BF16 = jnp.bfloat16

NX, NY, NZ = 4, 4, 8
PEERS = NX * NY
COLS, CX, CY, CZ = 8, 32, 16, 128
ROWS, TILES, RANK, TB = 4, 8, 32, 256
CONDUCTORS = 32
BND = 128
GROUP = PEERS
NEIGHBOURS = [(dx, dy) for dx in (-1, 0, 1) for dy in (-1, 0, 1) if (dx, dy) != (0, 0)]


def split(x):
    hi = x.astype(BF16).astype(F32)
    return hi, x - hi


def stacked(x):
    hi, lo = split(x)
    return jnp.concatenate([hi, lo], axis=0).astype(BF16)


def dot(a, b):
    return lax.dot_general(a, b, (((1,), (0,)), ((), ())), preferred_element_type=F32)


def dot_nt(a, b):
    return lax.dot_general(a, b, (((1,), (1,)), ((), ())), preferred_element_type=F32)


def face(step, size):
    if step == 0:
        return pl.ds(1, size), pl.ds(1, size)
    return (pl.ds(size, 1), pl.ds(0, 1)) if step > 0 else (pl.ds(1, 1), pl.ds(size + 1, 1))


def kernel(
    vol, scal, diag, bnd, cell, lab, left, right, near, slot,
    out, bnd_out, charges,
    vbuf, wbuf, tbuf, qbuf, obuf, sbuf, dbuf, bbuf, cellv, cells, labv, slots, leftb, rightb, nearb,
    xbuf, lbuf, ohz, pbuf, mbuf, rbuf, c1, c2, zsend, zlo, zhi, zcomb, trbuf,
    load_sem, vol_sem, out_sem, xs_sem, xr_sem, ls_sem, lr_sem, hs_sem, hr_sem,
    ms_sem, mr_sem, zs_sem, zr_sem, cs_sem, cr_sem,
):
    gx, gy, gz = lax.axis_index("gx"), lax.axis_index("gy"), lax.axis_index("gz")
    me2 = gx * NY + gy
    group = me2 // 2
    pos = lax.rem(gy, 2) * NZ + gz
    lane = lax.broadcasted_iota(jnp.int32, (COLS, CZ), 1)

    small = [(bnd, bbuf), (lab, labv), (cell, cells), (cell, cellv), (slot, slots),
             (scal, sbuf), (diag, dbuf), (right, rightb), (left, leftb), (near, nearb)]
    loads = [pltpu.make_async_copy(s, d, load_sem.at[i]) for i, (s, d) in enumerate(small)]
    (l_bnd, l_lab, l_cells, l_cellv, l_slot, l_scal, l_diag, l_right, l_left, l_near) = loads
    for l in (l_bnd, l_lab, l_scal):
        l.start()
    for c in range(COLS):
        pltpu.make_async_copy(vol.at[c], vbuf.at[:, c, :], vol_sem).start()
    for l in (l_cells, l_cellv, l_slot, l_right, l_left, l_near, l_diag):
        l.start()

    zero = jnp.zeros((COLS, CZ), F32)
    for x in (0, CX + 1):
        wbuf[x] = jnp.zeros((CY + 2, COLS, CZ), F32)
    for y in (0, CY + 1):
        wbuf[:, y] = jnp.zeros((CX + 2, COLS, CZ), F32)
    zlo[...] = jnp.zeros_like(zlo)
    zhi[...] = jnp.zeros_like(zhi)

    barrier = pltpu.get_barrier_semaphore()
    own_group = group == gz

    def greet(device):
        pl.semaphore_signal(barrier, inc=1, device_id=device, device_id_type=MESH)

    for p in range(GROUP):
        source = (gz // 2, lax.rem(gz, 2) * 2 + p // NZ, p % NZ)
        pl.when(jnp.logical_not(jnp.logical_and(own_group, pos == p)))(functools.partial(greet, source))
    for d in range(1, NZ):
        greet((gx, gy, lax.rem(gz + d, NZ)))
    for e in range(1, PEERS):
        other = lax.rem(me2 + e, PEERS)
        greet((other // NY, lax.rem(other, NY), gz))
    own = own_group.astype(jnp.int32)

    l_bnd.wait()
    l_lab.wait()
    pl.semaphore_wait(barrier, GROUP - own + (NZ - 1) + (PEERS - 1))

    def x_copy(t):
        return pltpu.make_async_remote_copy(
            bbuf, xbuf.at[pos], xs_sem.at[t], xr_sem,
            device_id=(t // NY, t % NY, group), device_id_type=MESH)

    x_self = pltpu.make_async_copy(bbuf, xbuf.at[pos], xr_sem)
    for t in range(GROUP):
        mine = jnp.logical_and(own_group, me2 == t)
        pl.when(jnp.logical_not(mine))(lambda t=t: x_copy(t).start())
    pl.when(own_group)(lambda: x_self.start())
    lbuf[gz] = labv[...]
    label_sends = [
        pltpu.make_async_remote_copy(
            labv, lbuf.at[gz], ls_sem, lr_sem,
            device_id=(gx, gy, lax.rem(gz + d, NZ)), device_id_type=MESH)
        for d in range(1, NZ)]
    for s in label_sends:
        s.start()

    l_scal.wait()
    pltpu.make_async_copy(vbuf, vbuf, vol_sem).wait()

    @pl.loop(0, CX)
    def _(x):
        for y in range(CY):
            s = sbuf[x, pl.ds(y, 1), :] * (1.0 / 6.0)
            wbuf[x + 1, y + 1] = jnp.broadcast_to(s, (COLS, CZ)) * vbuf[x * CY + y]

    halo = []
    for i, (dx, dy) in enumerate(NEIGHBOURS):
        (fx, tx), (fy, ty) = face(dx, CX), face(dy, CY)
        copy = pltpu.make_async_remote_copy(
            wbuf.at[fx, fy], wbuf.at[tx, ty], hs_sem.at[i], hr_sem.at[i],
            device_id=(lax.rem(gx + dx + NX, NX), lax.rem(gy + dy + NY, NY), gz), device_id_type=MESH)

        def within(a, b):
            return jnp.logical_and(jnp.logical_and(a >= 0, a < NX), jnp.logical_and(b >= 0, b < NY))

        to, come = within(gx + dx, gy + dy), within(gx - dx, gy - dy)
        pl.when(to)(copy.start)
        halo.append((copy, to, come))

    l_cells.wait()
    l_cellv.wait()

    def trace_one(k, acc):
        place = cells[0, k]
        row = vbuf[lax.shift_right_logical(place, 7)]
        turn = jnp.bitwise_and(k + CZ - jnp.bitwise_and(place, CZ - 1), CZ - 1)
        return jnp.where(lane == k, pltpu.roll(row, turn, 1), acc)

    traced = lax.fori_loop(0, BND, trace_one, zero, unroll=8)
    trbuf[...] = traced

    node = cellv[...]
    zk = jnp.bitwise_and(node, CZ - 1)
    onehot = (lax.broadcasted_iota(jnp.int32, (CZ, BND), 0) == zk).astype(F32).astype(BF16)
    ohz[:, pl.ds(0, BND)] = onehot
    ohz[:, pl.ds(BND, BND)] = onehot

    l_slot.wait()
    l_right.wait()
    l_left.wait()
    l_near.wait()
    pltpu.make_async_copy(xbuf, xbuf, xr_sem).wait()
    pieces = []
    for j in range(TILES):
        xj = jnp.concatenate([xbuf[2 * j], xbuf[2 * j + 1]], axis=1)
        hi, lo = split(xj)
        pieces.append(jnp.concatenate([hi, lo], axis=0))
    xall = jnp.concatenate(pieces, axis=0).astype(BF16)
    lane2 = lax.broadcasted_iota(jnp.int32, (COLS, TB), 1)
    for i in range(ROWS):
        proj = dot_nt(xall, rightb[i])
        acc = jnp.zeros((COLS, TB), F32)
        chosen = jnp.zeros((2 * COLS, TB), F32)
        for j in range(TILES):
            is_far = slots[i, j] < 0
            far = jnp.where(is_far, 1.0, 0.0).astype(F32)
            block = proj[16 * j:16 * j + 8] + proj[16 * j + 8:16 * j + 16]
            acc = jnp.where(lane2 // RANK == j, block * far, acc)
            chosen = chosen + pieces[j] * (1.0 - far)
        both = dot(stacked(acc), leftb[i]) + dot_nt(chosen.astype(BF16), nearb[i])
        part = -(both[:COLS] + both[COLS:])
        pbuf[2 * i] = part[:, :BND]
        pbuf[2 * i + 1] = part[:, BND:]

    pltpu.make_async_copy(lbuf.at[pl.ds(0, NZ - 1)], lbuf.at[pl.ds(0, NZ - 1)], lr_sem).wait()
    which = lax.broadcasted_iota(jnp.int32, (CONDUCTORS, BND), 0)

    def members(labels):
        return (which == labels).astype(F32).astype(BF16)

    gathered = dot_nt(stacked(trbuf[...]), members(labv[...]))
    for b in range(NZ):
        gathered = gathered + dot_nt(stacked(pbuf[b]), members(lbuf[b]))
    sums = jnp.concatenate([gathered[:COLS] + gathered[COLS:], jnp.zeros((COLS, BND - CONDUCTORS), F32)], axis=1)
    for b in range(NZ):
        mbuf[b, pl.ds(0, COLS), :] = pbuf[b]
        mbuf[b, pl.ds(COLS, COLS), :] = sums

    row_sends = []
    for d in range(1, NZ):
        other = lax.rem(gz + d, NZ)
        row_sends.append(pltpu.make_async_remote_copy(
            mbuf.at[other], rbuf.at[gz], ms_sem, mr_sem,
            device_id=(gx, gy, other), device_id_type=MESH))
    for s in row_sends:
        s.start()
    rbuf[gz] = mbuf[gz]

    for copy, to, come in halo:
        pl.when(come)(copy.wait_recv)

    @pl.loop(0, CX)
    def _(x):
        a = [wbuf[x, y] + wbuf[x + 2, y] for y in range(CY + 2)]
        w = [wbuf[x + 1, y] for y in range(CY + 2)]
        packed = zero
        for y in range(CY):
            p = a[y] + a[y + 2]
            t = (a[y + 1] + (w[y] + w[y + 2])) + 0.5 * p
            tbuf[x * CY + y] = t
            qbuf[x * CY + y] = 16.0 * w[y + 1] - p
            ends = jnp.logical_or(lane == (2 * y + CZ - 1) % CZ, lane == 2 * y)
            packed = jnp.where(ends, pltpu.roll(t, 2 * y, 1) if y else t, packed)
        quarter = lax.rem(x, 4)
        packed = pltpu.roll(packed, quarter * (2 * CY), 1)
        window = jnp.bitwise_and(lane + 1, CZ - 1) // (2 * CY) == quarter
        zsend[x // 4] = jnp.where(window, packed, zsend[x // 4])

    up, down = gz + 1 < NZ, gz > 0
    z_up = pltpu.make_async_remote_copy(
        zsend, zlo, zs_sem.at[0], zr_sem.at[0],
        device_id=(gx, gy, lax.rem(gz + 1, NZ)), device_id_type=MESH)
    z_down = pltpu.make_async_remote_copy(
        zsend, zhi, zs_sem.at[1], zr_sem.at[1],
        device_id=(gx, gy, lax.rem(gz + NZ - 1, NZ)), device_id_type=MESH)
    pl.when(up)(z_up.start)
    pl.when(down)(z_down.start)

    pltpu.make_async_copy(rbuf.at[pl.ds(0, NZ - 1)], rbuf.at[pl.ds(0, NZ - 1)], mr_sem).wait()
    total = rbuf[0]
    for b in range(1, NZ):
        total = total + rbuf[b]
    bnd_out[...] = trbuf[...] + total[:COLS]
    c1[...] = total[COLS:]
    c_sends = []
    for e in range(1, PEERS):
        other = lax.rem(me2 + e, PEERS)
        c_sends.append(pltpu.make_async_remote_copy(
            c1, c2.at[me2], cs_sem, cr_sem,
            device_id=(other // NY, lax.rem(other, NY), gz), device_id_type=MESH))
    for s in c_sends:
        s.start()
    c2[me2] = c1[...]

    l_diag.wait()
    pl.when(down)(z_up.wait_recv)
    pl.when(up)(z_down.wait_recv)
    odd = jnp.bitwise_and(lane, 1) == 1
    for g in range(CX // 4):
        zcomb[g] = jnp.where(odd, pltpu.roll(zlo[g], 2, 1), zhi[g])
    spots = jnp.broadcast_to(lax.shift_right_logical(node, 7), (COLS, BND))
    bhi, blo = split(bbuf[...])

    def second(x):
        rows = []
        for y in range(CY):
            here = spots == x * CY + y
            rows.append(jnp.concatenate([jnp.where(here, bhi, 0.0), jnp.where(here, blo, 0.0)], axis=1))
        extra = dot_nt(jnp.concatenate(rows, axis=0).astype(BF16), ohz[...])
        ends = pltpu.roll(zcomb[x // 4], lax.rem(4 - lax.rem(x, 4), 4) * (2 * CY), 1)
        for y in range(CY):
            t = tbuf[x * CY + y]
            r = pltpu.roll(ends, CZ - (2 * y + 1), 1)
            nb = jnp.where(lane == 0, r, pltpu.roll(t, 1, 1)) + jnp.where(lane == CZ - 1, r, pltpu.roll(t, CZ - 1, 1))
            s = jnp.broadcast_to(sbuf[x, pl.ds(y, 1), :], (COLS, CZ))
            d = jnp.broadcast_to(dbuf[x, pl.ds(y, 1), :], (COLS, CZ))
            base = s * (qbuf[x * CY + y] - nb) + d * vbuf[x * CY + y]
            obuf[x * CY + y] = base + extra[COLS * y:COLS * (y + 1)]

    chunk = 8
    for k in range(CX // chunk):
        pl.loop(k * chunk, (k + 1) * chunk)(second)
        rows = pl.ds(k * chunk * CY, chunk * CY)
        for c in range(COLS):
            pltpu.make_async_copy(obuf.at[rows, c, :], out.at[c, rows, :], out_sem).start()

    pltpu.make_async_copy(c2.at[pl.ds(0, PEERS - 1)], c2.at[pl.ds(0, PEERS - 1)], cr_sem).wait()
    total = c2[0]
    for b in range(1, PEERS):
        total = total + c2[b]
    charges[...] = total[:, :CONDUCTORS] * (CONDUCTORS / (BND * NX * NY * NZ)) ** 0.5

    for t in range(GROUP):
        mine = jnp.logical_and(own_group, me2 == t)
        pl.when(jnp.logical_not(mine))(lambda t=t: x_copy(t).wait_send())
    for s in label_sends + row_sends + c_sends:
        s.wait_send()
    for copy, to, come in halo:
        pl.when(to)(copy.wait_send)
    pl.when(up)(z_up.wait_send)
    pl.when(down)(z_down.wait_send)
    pltpu.make_async_copy(obuf, obuf, out_sem).wait()


def shards(vol, scal, diag, bnd, cell, lab, left, right, near, slot):
    any_spec = pl.BlockSpec(memory_space=pl.ANY)
    vmem_spec = pl.BlockSpec(memory_space=pltpu.VMEM)
    nodes = CX * CY
    field = (nodes, COLS, CZ)
    dma = pltpu.SemaphoreType.DMA
    out, bnd_out, charges = pl.pallas_call(
        kernel,
        out_shape=(
            jax.ShapeDtypeStruct((COLS, nodes, CZ), F32),
            jax.ShapeDtypeStruct((COLS, BND), F32),
            jax.ShapeDtypeStruct((COLS, CONDUCTORS), F32),
        ),
        in_specs=[any_spec] * 10,
        out_specs=(any_spec, vmem_spec, vmem_spec),
        scratch_shapes=[
            pltpu.VMEM(field, F32),
            pltpu.VMEM((CX + 2, CY + 2, COLS, CZ), F32),
            pltpu.VMEM(field, F32),
            pltpu.VMEM(field, F32),
            pltpu.VMEM(field, F32),
            pltpu.VMEM((CX, CY, CZ), F32),
            pltpu.VMEM((CX, CY, CZ), F32),
            pltpu.VMEM((COLS, BND), F32),
            pltpu.VMEM((1, BND), jnp.int32),
            pltpu.SMEM((1, BND), jnp.int32),
            pltpu.VMEM((1, BND), jnp.int32),
            pltpu.SMEM((ROWS, TILES), jnp.int32),
            pltpu.VMEM((ROWS, TB, TB), BF16),
            pltpu.VMEM((ROWS, TB, TB), BF16),
            pltpu.VMEM((ROWS, TB, TB), BF16),
            pltpu.VMEM((GROUP, COLS, BND), F32),
            pltpu.VMEM((NZ, 1, BND), jnp.int32),
            pltpu.VMEM((CZ, 2 * BND), BF16),
            pltpu.VMEM((NZ, COLS, BND), F32),
            pltpu.VMEM((NZ, 2 * COLS, BND), F32),
            pltpu.VMEM((NZ, 2 * COLS, BND), F32),
            pltpu.VMEM((COLS, BND), F32),
            pltpu.VMEM((PEERS, COLS, BND), F32),
            pltpu.VMEM((CX // 4, COLS, CZ), F32),
            pltpu.VMEM((CX // 4, COLS, CZ), F32),
            pltpu.VMEM((CX // 4, COLS, CZ), F32),
            pltpu.VMEM((CX // 4, COLS, CZ), F32),
            pltpu.VMEM((COLS, BND), F32),
            dma((10,)), dma, dma, dma((GROUP,)), dma, dma, dma, dma((8,)), dma((8,)),
            dma, dma, dma((2,)), dma((2,)), dma, dma,
        ],
        compiler_params=pltpu.CompilerParams(
            collective_id=0, has_side_effects=True, vmem_limit_bytes=40 * 1024 * 1024),
    )(
        vol.reshape(COLS, nodes, CZ), scal, diag, bnd, cell.reshape(1, BND), lab.reshape(1, BND),
        left.reshape(ROWS, TB, TB), right.reshape(ROWS, TB, TB), near.reshape(ROWS, TB, TB), slot,
    )
    return out.reshape(vol.shape), bnd_out, charges.T


def solution(mesh):
    in_specs = (
        P(None, "gx", "gy", "gz"),
        P("gx", "gy", "gz"),
        P("gx", "gy", "gz"),
        P(None, ("gx", "gy", "gz")),
        P(("gx", "gy", "gz")),
        P(("gx", "gy", "gz")),
        P(("gx", "gy"), "gz", None, None),
        P(("gx", "gy"), "gz", None, None),
        P(("gx", "gy"), "gz", None, None),
        P(("gx", "gy"), "gz"),
    )
    out_specs = (P(None, "gx", "gy", "gz"), P(None, ("gx", "gy", "gz")), P())
    return jax.shard_map(shards, mesh=mesh, in_specs=in_specs, out_specs=out_specs, check_vma=False)
```

time: 563 us -> 45.4 us (0.08)
  blocking collectives: 420 us -> 0 us
  local copies, waits for them, and re-layouts: 79.4 us -> 11.8 us
  other arithmetic: 40.9 us -> 0 us
  Pallas kernels: 0 us -> 32.5 us
  starting transfers between devices: 15 us -> 0 us
    all_gather x1 -> x0, blocking collectives: 279 us -> none  [shards(): gathered = lax.all_gather(bnd_field, ('gx', 'gy', 'gz'), axis=1, tiled=True)]
    psum x2 -> x0, blocking collectives: 141 us -> none  [the longest x1 108 us: shards(): lax.psum(local_sum, ('gx', 'gy', 'gz')) * (CONDUCTORS / total_nodes) ** 0.5]
    pallas_call x0 -> x1, Pallas kernels: none -> 32.5 us  [shards(): pl.pallas_call(kernel, out_shape=(jax.ShapeDtypeStruct((COLS, nodes, CZ),...]
    unnamed x22 -> x23, local copies, waits for them, and re-layouts: 37.8 us -> 11.8 us
    scatter-add x1 -> x0, other arithmetic: 22.7 us -> none  [shards(): vol_out = vol_base.reshape(columns, size_x * size_y * size_z).at[:, bnd_c...]
    add x1 -> x0, local copies, waits for them, and re-layouts: 16.2 us -> none  [shards(): vol_base = scaling * stiffness(scaling * vol_field) + diag_shift * vol_field]
    ppermute x6 -> x0, starting transfers between devices: 15 us -> none  [the longest x3 10.4 us: extended(): before = lax.ppermute(last, axis, up)]
    gather x1 -> x0, local copies, waits for them, and re-layouts: 11.2 us -> none  [shards(): jnp.take(vol_field.reshape(columns, size_x * size_y * size_z), bnd_cell,...]
  transfers between devices with their start and end apart: 6 -> 0, of which waited for: 0 -> 0; matrix products, arithmetic and copies ran while one was open for 7% -> 0% of each run, Pallas kernels for 0% -> 0%
where the time goes in v1:
time: 45.4 us; the launch traced here: 44.9 us
  Pallas kernels  32.5 us (72%)
  local copies, waits for them, and re-layouts  11.8 us (26%)
  between operations  0.66 us (1%)
    pallas_call x1, Pallas kernels, shards(): pl.pallas_call(kernel, out_shape=(jax.ShapeDtypeStruct((COLS, nodes, CZ),...  32.5 us
    unnamed x23, local copies, waits for them, and re-layouts  11.8 us

profile of v1, /device:TPU:1, one launch (start us, length us, event | category | flops | bytes accessed | tf_op | source)
XLA Modules:
  0.0 44.9 jit_solution(12417157599786144287)
XLA Ops:
  0.6 0.0 copy-start
  0.6 1.6 %copy-done = f32[8,32,16,128]{3,2,1,0:T(8,128)S(1)} copy-done((f32[8,32,16,128]{3,2,1,0:T(8,128)S(1)}, f32[8,32,16,128]{3,2,1,0:T(8,128)}, u32[]{:S(2)}) %copy-start) | copy-done | bytes 2097176
  2.2 0.0 copy-start.1
  2.2 1.0 %copy-done.1 = bf16[4,8,32,256]{3,2,1,0:T(8,128)(2,1)S(1)} copy-done((bf16[4,8,32,256]{3,2,1,0:T(8,128)(2,1)S(1)}, bf16[4,8,32,256]{3,2,1,0:T(8,128)(2,1)}, u32[]{:S(2)}) %copy-start.1) | copy-done | bytes 524312
  3.3 0.0 copy-start.2
  3.3 1.0 %copy-done.2 = bf16[4,8,32,256]{3,2,1,0:T(8,128)(2,1)S(1)} copy-done((bf16[4,8,32,256]{3,2,1,0:T(8,128)(2,1)S(1)}, bf16[4,8,32,256]{3,2,1,0:T(8,128)(2,1)}, u32[]{:S(2)}) %copy-start.2) | copy-done | bytes 524312
  4.3 0.0 copy-start.3
  4.3 1.0 %copy-done.3 = bf16[4,1,256,256]{3,2,1,0:T(8,128)(2,1)S(1)} copy-done((bf16[4,1,256,256]{3,2,1,0:T(8,128)(2,1)S(1)}, bf16[4,1,256,256]{3,2,1,0:T(8,128)(2,1)}, u32[]{:S(2)}) %copy-start.3) | copy-done | bytes 524312
  5.4 0.0 copy-start.4
  5.4 0.9 %copy-done.4 = f32[32,16,128]{2,1,0:T(8,128)S(1)} copy-done((f32[32,16,128]{2,1,0:T(8,128)S(1)}, f32[32,16,128]{2,1,0:T(8,128)}, u32[]{:S(2)}) %copy-start.4) | copy-done | bytes 262168
  6.3 0.0 copy-start.5
  6.3 0.9 %copy-done.5 = f32[32,16,128]{2,1,0:T(8,128)S(1)} copy-done((f32[32,16,128]{2,1,0:T(8,128)S(1)}, f32[32,16,128]{2,1,0:T(8,128)}, u32[]{:S(2)}) %copy-start.5) | copy-done | bytes 262168
  7.3 0.0 copy-start.6
  7.3 0.7 %copy-done.6 = f32[8,128]{1,0:T(8,128)S(1)} copy-done((f32[8,128]{1,0:T(8,128)S(1)}, f32[8,128]{1,0:T(8,128)}, u32[]{:S(2)}) %copy-start.6) | copy-done | bytes 4120
  7.9 0.0 copy-start.7
  7.9 0.7 %copy-done.7 = s32[4,8]{1,0:T(4,128)S(1)} copy-done((s32[4,8]{1,0:T(4,128)S(1)}, s32[4,8]{1,0:T(4,128)}, u32[]{:S(2)}) %copy-start.7) | copy-done | bytes 152
  8.6 0.0 copy-start.8
  8.6 0.7 %copy-done.8 = s32[128]{0:T(128)S(1)} copy-done((s32[128]{0:T(128)S(1)}, s32[128]{0:T(128)}, u32[]{:S(2)}) %copy-start.8) | copy-done | bytes 536
  9.3 0.0 copy-start.9
  9.3 0.7 %copy-done.9 = s32[128]{0:T(128)S(1)} copy-done((s32[128]{0:T(128)S(1)}, s32[128]{0:T(128)}, u32[]{:S(2)}) %copy-start.9) | copy-done | bytes 536
  9.9 32.5 %shard_map.121 = (f32[8,512,128]{2,1,0:T(8,128)S(1)}, f32[8,128]{1,0:T(8,128)S(1)}, f32[8,32]{1,0:T(8,128)S(1)}) custom-call(f32[8,512,128]{2,1,0:T(8,128)S(1)} %bitcast.8, f32[32,16,128]{2,1,0:T(8,128)S(1)} %copy-done.4, f32[32,16,128]{2,1,0:T(8,128)S(1)} %copy-done.5, f32[8,128]{1,0:T(8,128)S(1)} %copy-done.6, s32[1,128]{1,0:T(1,128)S(1)} %bitcast.14, ...), custom_call_target="tpu_custom_call" | custom-call | tf_op jit(solution)/shard_map/pallas_call | solution.py:314
  42.4 1.3 %copy.16 = f32[8,32,16,128]{3,2,1,0:T(8,128)} copy(f32[8,32,16,128]{3,2,1,0:T(8,128)S(1)} %bitcast.9) | data formatting | bytes 4194304
  43.8 0.6 %copy.17 = f32[8,128]{1,0:T(8,128)} copy(f32[8,128]{1,0:T(8,128)S(1)} %get-tuple-element.13) | data formatting | bytes 8192
  44.3 0.6 %copy.18 = f32[32,8]{0,1:T(8,128)} copy(f32[32,8]{0,1:T(8,128)S(1)} %bitcast.13) | data formatting | bytes 2048
Async XLA Ops:
  0.6 1.6 %copy-start = (f32[8,32,16,128]{3,2,1,0:T(8,128)S(1)}, f32[8,32,16,128]{3,2,1,0:T(8,128)}, u32[]{:S(2)}) copy-start(f32[8,32,16,128]{3,2,1,0:T(8,128)} %param.10) | copy-start | bytes 6291460
  2.2 1.0 %copy-start.1 = (bf16[4,8,32,256]{3,2,1,0:T(8,128)(2,1)S(1)}, bf16[4,8,32,256]{3,2,1,0:T(8,128)(2,1)}, u32[]{:S(2)}) copy-start(bf16[4,8,32,256]{3,2,1,0:T(8,128)(2,1)} %param.16) | copy-start | bytes 1572868
  3.3 1.0 %copy-start.2 = (bf16[4,8,32,256]{3,2,1,0:T(8,128)(2,1)S(1)}, bf16[4,8,32,256]{3,2,1,0:T(8,128)(2,1)}, u32[]{:S(2)}) copy-start(bf16[4,8,32,256]{3,2,1,0:T(8,128)(2,1)} %param.17) | copy-start | bytes 1572868
  4.3 1.0 %copy-start.3 = (bf16[4,1,256,256]{3,2,1,0:T(8,128)(2,1)S(1)}, bf16[4,1,256,256]{3,2,1,0:T(8,128)(2,1)}, u32[]{:S(2)}) copy-start(bf16[4,1,256,256]{3,2,1,0:T(8,128)(2,1)} %param.18) | copy-start | bytes 1572868
  5.4 0.9 %copy-start.4 = (f32[32,16,128]{2,1,0:T(8,128)S(1)}, f32[32,16,128]{2,1,0:T(8,128)}, u32[]{:S(2)}) copy-start(f32[32,16,128]{2,1,0:T(8,128)} %scal.1) | copy-start | bytes 786436
  6.3 0.9 %copy-start.5 = (f32[32,16,128]{2,1,0:T(8,128)S(1)}, f32[32,16,128]{2,1,0:T(8,128)}, u32[]{:S(2)}) copy-start(f32[32,16,128]{2,1,0:T(8,128)} %diag.1) | copy-start | bytes 786436
  7.3 0.7 %copy-start.6 = (f32[8,128]{1,0:T(8,128)S(1)}, f32[8,128]{1,0:T(8,128)}, u32[]{:S(2)}) copy-start(f32[8,128]{1,0:T(8,128)} %bnd.1) | copy-start | bytes 12292
  7.9 0.7 %copy-start.7 = (s32[4,8]{1,0:T(4,128)S(1)}, s32[4,8]{1,0:T(4,128)}, u32[]{:S(2)}) copy-start(s32[4,8]{1,0:T(4,128)} %slot.1) | copy-start | bytes 388
  8.6 0.7 %copy-start.8 = (s32[128]{0:T(128)S(1)}, s32[128]{0:T(128)}, u32[]{:S(2)}) copy-start(s32[128]{0:T(128)} %param.14) | copy-start | bytes 1540
  9.3 0.7 %copy-start.9 = (s32[128]{0:T(128)S(1)}, s32[128]{0:T(128)}, u32[]{:S(2)}) copy-start(s32[128]{0:T(128)} %param.15) | copy-start | bytes 1540

commit v2 on v1

v2 whole, which is shorter than its diff:
```python
import functools

import jax
import jax.numpy as jnp
from jax import lax
from jax.experimental import pallas as pl
from jax.experimental.pallas import tpu as pltpu
from jax.sharding import PartitionSpec as P

MESH = pl.DeviceIdType.MESH
F32 = jnp.float32
BF16 = jnp.bfloat16

NX, NY, NZ = 4, 4, 8
PEERS = NX * NY
COLS, CX, CY, CZ = 8, 32, 16, 128
ROWS, TILES, RANK, TB = 4, 8, 32, 256
CONDUCTORS = 32
BND = 128
GROUP = PEERS
NEIGHBOURS = [(dx, dy) for dx in (-1, 0, 1) for dy in (-1, 0, 1) if (dx, dy) != (0, 0)]


def split(x):
    hi = x.astype(BF16).astype(F32)
    return hi, x - hi


def stacked(x):
    hi, lo = split(x)
    return jnp.concatenate([hi, lo], axis=0).astype(BF16)


def dot(a, b):
    return lax.dot_general(a, b, (((1,), (0,)), ((), ())), preferred_element_type=F32)


def dot_nt(a, b):
    return lax.dot_general(a, b, (((1,), (1,)), ((), ())), preferred_element_type=F32)


def face(step, size):
    if step == 0:
        return pl.ds(1, size), pl.ds(1, size)
    return (pl.ds(size, 1), pl.ds(0, 1)) if step > 0 else (pl.ds(1, 1), pl.ds(size + 1, 1))


GX = 8


def scale_pass(sbuf, vbuf, wbuf):
    @pl.loop(0, CX)
    def _(x):
        for y in range(CY):
            s = sbuf[x, pl.ds(y, 1), :] * (1.0 / 6.0)
            wbuf[x + 1, y + 1] = jnp.broadcast_to(s, (COLS, CZ)) * vbuf[x * CY + y]


def line_weights(wz, ez):
    z = lax.broadcasted_iota(jnp.int32, (CZ, CZ), 0)
    n = lax.broadcasted_iota(jnp.int32, (CZ, CZ), 1)
    near = jnp.logical_or(z == n + 1, z == n - 1)
    first = jnp.bitwise_and(n, CX) == 0
    ends = jnp.logical_or(jnp.logical_and(z == 0, first), jnp.logical_and(z == CZ - 1, jnp.logical_not(first)))
    from_above = jnp.bitwise_and(z, CX) == 0
    land = jnp.logical_or(jnp.logical_and(n == CZ - 1, from_above), jnp.logical_and(n == 0, jnp.logical_not(from_above)))

    def ones(mask):
        return mask.astype(F32).astype(BF16)

    for piece in range(2):
        rows = pl.ds(piece * CZ, CZ)
        wz[rows, pl.ds(0, CZ)] = ones(near)
        wz[rows, pl.ds(CZ, CZ)] = ones(ends)
        ez[rows, :] = ones(land)


def node_columns(cellv, ohz):
    zk = jnp.bitwise_and(cellv[...], CZ - 1)
    onehot = (lax.broadcasted_iota(jnp.int32, (CZ, BND), 0) == zk).astype(F32).astype(BF16)
    ohz[:, pl.ds(0, BND)] = onehot
    ohz[:, pl.ds(BND, BND)] = onehot


def node_pass(bbuf, cellv, ohz, vbuf, dbuf, lhs, obuf):
    spots = jnp.broadcast_to(lax.shift_right_logical(cellv[...], 7), (COLS, BND))
    pieces = split(bbuf[...])

    @pl.loop(0, CX)
    def _(x):
        for y in range(0, CY, 2):
            here = [spots == x * CY + y, spots == x * CY + y + 1]
            for p in range(2):
                both = jnp.concatenate([jnp.where(h, pieces[p], 0.0) for h in here], axis=0)
                lhs[x, pl.ds(COLS * y, 2 * COLS), pl.ds(p * BND, BND)] = both.astype(BF16)

    @pl.loop(0, CX // GX)
    def _(g):
        extra = dot_nt(lhs[pl.ds(g * GX, GX)].reshape(GX * CY * COLS, 2 * BND), ohz[...])
        for i in range(GX):
            for y in range(CY):
                x = g * GX + i
                d = jnp.broadcast_to(dbuf[x, pl.ds(y, 1), :], (COLS, CZ))
                k = (i * CY + y) * COLS
                obuf[x * CY + y] = d * vbuf[x * CY + y] + extra[k:k + COLS]


def line_pass(wbuf, lhs, qbuf):
    @pl.loop(0, CX)
    def _(x):
        a = [wbuf[x, y] + wbuf[x + 2, y] for y in range(CY + 2)]
        w = [wbuf[x + 1, y] for y in range(CY + 2)]
        for y0 in range(0, CY, 2):
            ts = []
            for y in (y0, y0 + 1):
                p = a[y] + a[y + 2]
                ts.append((a[y + 1] + (w[y] + w[y + 2])) + 0.5 * p)
                qbuf[x * CY + y] = 16.0 * w[y + 1] - p
            t = jnp.concatenate(ts, axis=0)
            hi = t.astype(BF16)
            lhs[x, pl.ds(COLS * y0, 2 * COLS), pl.ds(0, CZ)] = hi
            lhs[x, pl.ds(COLS * y0, 2 * COLS), pl.ds(CZ, CZ)] = (t - hi.astype(F32)).astype(BF16)


def sum_pass(lhs, wz, qbuf, sbuf, obuf, zsend, lane):
    spot = jnp.bitwise_and(lane, CX - 1)
    half = lax.shift_right_logical(lane, 6)

    @pl.loop(0, CX // GX)
    def _(g):
        r = dot(lhs[pl.ds(g * GX, GX)].reshape(GX * CY * COLS, 2 * CZ), wz[...])
        ends = [zsend[y] for y in range(CY // 2)]
        for i in range(GX):
            x = g * GX + i
            mine = [jnp.logical_and(half == h, spot == x) for h in range(2)]
            for y in range(CY):
                k = (i * CY + y) * COLS
                s = jnp.broadcast_to(sbuf[x, pl.ds(y, 1), :], (COLS, CZ))
                obuf[x * CY + y] = obuf[x * CY + y] + s * (qbuf[x * CY + y] - r[k:k + COLS, :CZ])
                e = y % (CY // 2)
                ends[e] = jnp.where(mine[y // (CY // 2)], r[k:k + COLS, CZ:], ends[e])
        for y in range(CY // 2):
            zsend[y] = ends[y]


def end_rows(zlo, zhi, zc, lane):
    above = jnp.bitwise_and(lane, CX) == 0
    for y in range(0, CY, 2):
        e = y % (CY // 2)
        both = []
        for k in (e, e + 1):
            row = jnp.where(above, zhi[k], zlo[k])
            both.append(jnp.where(lax.shift_right_logical(lane, 6) == y // (CY // 2), row, 0.0))
        z = jnp.concatenate(both, axis=0)
        hi = z.astype(BF16)
        zc[pl.ds(COLS * y, 2 * COLS), pl.ds(0, CZ)] = hi
        zc[pl.ds(COLS * y, 2 * COLS), pl.ds(CZ, CZ)] = (z - hi.astype(F32)).astype(BF16)


def end_pass(k, chunk, zc, ez, sbuf, obuf):
    lane2 = jnp.bitwise_and(lax.broadcasted_iota(jnp.int32, (2 * COLS, 2 * CZ), 1), CX - 1)

    @pl.loop(k * (chunk // GX), (k + 1) * (chunk // GX))
    def _(g):
        rows = []
        for i in range(GX):
            here = (lane2 == g * GX + i).astype(F32).astype(BF16)
            for y in range(0, CY, 2):
                rows.append(zc[pl.ds(COLS * y, 2 * COLS), :] * here)
        h = dot(jnp.concatenate(rows, axis=0), ez[...])
        for i in range(GX):
            x = g * GX + i
            for y in range(CY):
                q = (i * CY + y) * COLS
                s = jnp.broadcast_to(sbuf[x, pl.ds(y, 1), :], (COLS, CZ))
                obuf[x * CY + y] = obuf[x * CY + y] - s * h[q:q + COLS]


def trace_nodes(cells, vbuf, lane):
    def trace_one(k, acc):
        place = cells[0, k]
        row = vbuf[lax.shift_right_logical(place, 7)]
        turn = jnp.bitwise_and(k + CZ - jnp.bitwise_and(place, CZ - 1), CZ - 1)
        return jnp.where(lane == k, pltpu.roll(row, turn, 1), acc)

    return lax.fori_loop(0, BND, trace_one, jnp.zeros((COLS, CZ), F32), unroll=8)


def tile_products(xbuf, slots, rightb, leftb, nearb, pbuf):
    pieces = []
    for j in range(TILES):
        xj = jnp.concatenate([xbuf[2 * j], xbuf[2 * j + 1]], axis=1)
        hi, lo = split(xj)
        pieces.append(jnp.concatenate([hi, lo], axis=0))
    xall = jnp.concatenate(pieces, axis=0).astype(BF16)
    lane2 = lax.broadcasted_iota(jnp.int32, (COLS, TB), 1)
    for i in range(ROWS):
        proj = dot_nt(xall, rightb[i])
        acc = jnp.zeros((COLS, TB), F32)
        chosen = jnp.zeros((2 * COLS, TB), F32)
        for j in range(TILES):
            is_far = slots[i, j] < 0
            far = jnp.where(is_far, 1.0, 0.0).astype(F32)
            block = proj[16 * j:16 * j + 8] + proj[16 * j + 8:16 * j + 16]
            acc = jnp.where(lane2 // RANK == j, block * far, acc)
            chosen = chosen + pieces[j] * (1.0 - far)
        both = dot(stacked(acc), leftb[i]) + dot_nt(chosen.astype(BF16), nearb[i])
        part = -(both[:COLS] + both[COLS:])
        pbuf[2 * i] = part[:, :BND]
        pbuf[2 * i + 1] = part[:, BND:]


def conductor_sums(trbuf, labv, lbuf, pbuf, mbuf):
    which = lax.broadcasted_iota(jnp.int32, (CONDUCTORS, BND), 0)

    def members(labels):
        return (which == labels).astype(F32).astype(BF16)

    gathered = dot_nt(stacked(trbuf[...]), members(labv[...]))
    for b in range(NZ):
        gathered = gathered + dot_nt(stacked(pbuf[b]), members(lbuf[b]))
    sums = jnp.concatenate([gathered[:COLS] + gathered[COLS:], jnp.zeros((COLS, BND - CONDUCTORS), F32)], axis=1)
    for b in range(NZ):
        mbuf[b, pl.ds(0, COLS), :] = pbuf[b]
        mbuf[b, pl.ds(COLS, COLS), :] = sums


def kernel(
    vol, scal, diag, bnd, cell, lab, left, right, near, slot,
    obuf, bnd_out, charges,
    vbuf, wbuf, qbuf, lhs, sbuf, dbuf, bbuf, cellv, cells, labv, slots, leftb, rightb, nearb,
    xbuf, lbuf, ohz, wz, ez, zc, pbuf, mbuf, rbuf, c1, c2, zsend, zlo, zhi, trbuf,
    load_sem, vol_sem, xs_sem, xr_sem, ls_sem, lr_sem, hs_sem, hr_sem,
    ms_sem, mr_sem, zs_sem, zr_sem, cs_sem, cr_sem,
):
    gx, gy, gz = lax.axis_index("gx"), lax.axis_index("gy"), lax.axis_index("gz")
    me2 = gx * NY + gy
    group = me2 // 2
    pos = lax.rem(gy, 2) * NZ + gz
    lane = lax.broadcasted_iota(jnp.int32, (COLS, CZ), 1)

    small = [(bnd, bbuf), (lab, labv), (cell, cells), (cell, cellv), (slot, slots),
             (scal, sbuf), (diag, dbuf), (right, rightb), (left, leftb), (near, nearb)]
    loads = [pltpu.make_async_copy(s, d, load_sem.at[i]) for i, (s, d) in enumerate(small)]
    (l_bnd, l_lab, l_cells, l_cellv, l_slot, l_scal, l_diag, l_right, l_left, l_near) = loads
    for l in (l_bnd, l_lab, l_scal):
        l.start()
    for c in range(COLS):
        pltpu.make_async_copy(vol.at[c], vbuf.at[:, c, :], vol_sem).start()
    for l in (l_cells, l_cellv, l_slot, l_right, l_left, l_near, l_diag):
        l.start()

    zero = jnp.zeros((COLS, CZ), F32)
    for x in (0, CX + 1):
        wbuf[x] = jnp.zeros((CY + 2, COLS, CZ), F32)
    for y in (0, CY + 1):
        wbuf[:, y] = jnp.zeros((CX + 2, COLS, CZ), F32)
    zlo[...] = jnp.zeros_like(zlo)
    zhi[...] = jnp.zeros_like(zhi)
    zsend[...] = jnp.zeros_like(zsend)

    barrier = pltpu.get_barrier_semaphore()
    own_group = group == gz

    def greet(device):
        pl.semaphore_signal(barrier, inc=1, device_id=device, device_id_type=MESH)

    for p in range(GROUP):
        source = (gz // 2, lax.rem(gz, 2) * 2 + p // NZ, p % NZ)
        pl.when(jnp.logical_not(jnp.logical_and(own_group, pos == p)))(functools.partial(greet, source))
    for d in range(1, NZ):
        greet((gx, gy, lax.rem(gz + d, NZ)))
    for e in range(1, PEERS):
        other = lax.rem(me2 + e, PEERS)
        greet((other // NY, lax.rem(other, NY), gz))
    own = own_group.astype(jnp.int32)

    l_bnd.wait()
    l_lab.wait()
    pl.semaphore_wait(barrier, GROUP - own + (NZ - 1) + (PEERS - 1))

    def x_copy(t):
        return pltpu.make_async_remote_copy(
            bbuf, xbuf.at[pos], xs_sem.at[t], xr_sem,
            device_id=(t // NY, t % NY, group), device_id_type=MESH)

    x_self = pltpu.make_async_copy(bbuf, xbuf.at[pos], xr_sem)
    for t in range(GROUP):
        mine = jnp.logical_and(own_group, me2 == t)
        pl.when(jnp.logical_not(mine))(lambda t=t: x_copy(t).start())
    pl.when(own_group)(lambda: x_self.start())
    lbuf[gz] = labv[...]
    label_sends = [
        pltpu.make_async_remote_copy(
            labv, lbuf.at[gz], ls_sem, lr_sem,
            device_id=(gx, gy, lax.rem(gz + d, NZ)), device_id_type=MESH)
        for d in range(1, NZ)]
    for s in label_sends:
        s.start()

    l_scal.wait()
    pltpu.make_async_copy(vbuf, vbuf, vol_sem).wait()

    scale_pass(sbuf, vbuf, wbuf)

    halo = []
    for i, (dx, dy) in enumerate(NEIGHBOURS):
        (fx, tx), (fy, ty) = face(dx, CX), face(dy, CY)
        copy = pltpu.make_async_remote_copy(
            wbuf.at[fx, fy], wbuf.at[tx, ty], hs_sem.at[i], hr_sem.at[i],
            device_id=(lax.rem(gx + dx + NX, NX), lax.rem(gy + dy + NY, NY), gz), device_id_type=MESH)

        def within(a, b):
            return jnp.logical_and(jnp.logical_and(a >= 0, a < NX), jnp.logical_and(b >= 0, b < NY))

        to, come = within(gx + dx, gy + dy), within(gx - dx, gy - dy)
        pl.when(to)(copy.start)
        halo.append((copy, to, come))

    l_cells.wait()
    l_cellv.wait()

    trbuf[...] = trace_nodes(cells, vbuf, lane)
    line_weights(wz, ez)
    node_columns(cellv, ohz)
    l_diag.wait()
    node_pass(bbuf, cellv, ohz, vbuf, dbuf, lhs, obuf)

    l_slot.wait()
    l_right.wait()
    l_left.wait()
    l_near.wait()
    pltpu.make_async_copy(xbuf, xbuf, xr_sem).wait()
    tile_products(xbuf, slots, rightb, leftb, nearb, pbuf)
    pltpu.make_async_copy(lbuf.at[pl.ds(0, NZ - 1)], lbuf.at[pl.ds(0, NZ - 1)], lr_sem).wait()
    conductor_sums(trbuf, labv, lbuf, pbuf, mbuf)

    row_sends = []
    for d in range(1, NZ):
        other = lax.rem(gz + d, NZ)
        row_sends.append(pltpu.make_async_remote_copy(
            mbuf.at[other], rbuf.at[gz], ms_sem, mr_sem,
            device_id=(gx, gy, other), device_id_type=MESH))
    for s in row_sends:
        s.start()
    rbuf[gz] = mbuf[gz]

    for copy, to, come in halo:
        pl.when(come)(copy.wait_recv)

    line_pass(wbuf, lhs, qbuf)
    sum_pass(lhs, wz, qbuf, sbuf, obuf, zsend, lane)

    up, down = gz + 1 < NZ, gz > 0
    z_up = pltpu.make_async_remote_copy(
        zsend, zlo, zs_sem.at[0], zr_sem.at[0],
        device_id=(gx, gy, lax.rem(gz + 1, NZ)), device_id_type=MESH)
    z_down = pltpu.make_async_remote_copy(
        zsend, zhi, zs_sem.at[1], zr_sem.at[1],
        device_id=(gx, gy, lax.rem(gz + NZ - 1, NZ)), device_id_type=MESH)
    pl.when(up)(z_up.start)
    pl.when(down)(z_down.start)

    pltpu.make_async_copy(rbuf.at[pl.ds(0, NZ - 1)], rbuf.at[pl.ds(0, NZ - 1)], mr_sem).wait()
    total = rbuf[0]
    for b in range(1, NZ):
        total = total + rbuf[b]
    bnd_out[...] = trbuf[...] + total[:COLS]
    c1[...] = total[COLS:]
    c_sends = []
    for e in range(1, PEERS):
        other = lax.rem(me2 + e, PEERS)
        c_sends.append(pltpu.make_async_remote_copy(
            c1, c2.at[me2], cs_sem, cr_sem,
            device_id=(other // NY, lax.rem(other, NY), gz), device_id_type=MESH))
    for s in c_sends:
        s.start()
    c2[me2] = c1[...]

    pl.when(down)(z_up.wait_recv)
    pl.when(up)(z_down.wait_recv)
    end_rows(zlo, zhi, zc, lane)
    end_pass(0, CX, zc, ez, sbuf, obuf)

    pltpu.make_async_copy(c2.at[pl.ds(0, PEERS - 1)], c2.at[pl.ds(0, PEERS - 1)], cr_sem).wait()
    total = c2[0]
    for b in range(1, PEERS):
        total = total + c2[b]
    charges[...] = total[:, :CONDUCTORS] * (CONDUCTORS / (BND * NX * NY * NZ)) ** 0.5

    for t in range(GROUP):
        mine = jnp.logical_and(own_group, me2 == t)
        pl.when(jnp.logical_not(mine))(lambda t=t: x_copy(t).wait_send())
    for s in label_sends + row_sends + c_sends:
        s.wait_send()
    for copy, to, come in halo:
        pl.when(to)(copy.wait_send)
    pl.when(up)(z_up.wait_send)
    pl.when(down)(z_down.wait_send)


def deliver(field, rows, sums, out, bnd_out, charges, sem, small_sem):
    copies = [pltpu.make_async_copy(field.at[:, c, :], out.at[c], sem) for c in range(COLS)]
    copies.append(pltpu.make_async_copy(rows, bnd_out, small_sem.at[0]))
    copies.append(pltpu.make_async_copy(sums, charges, small_sem.at[1]))
    for c in copies:
        c.start()
    pltpu.make_async_copy(field, field, sem).wait()
    copies[-2].wait()
    copies[-1].wait()


def shards(vol, scal, diag, bnd, cell, lab, left, right, near, slot):
    nodes = CX * CY
    field = (nodes, COLS, CZ)
    dma = pltpu.SemaphoreType.DMA
    hbm_spec = pl.BlockSpec(memory_space=pltpu.HBM)
    vmem_spec = pl.BlockSpec(memory_space=pltpu.VMEM)
    operands = (
        vol.reshape(COLS, nodes, CZ), scal, diag, bnd, cell.reshape(1, BND), lab.reshape(1, BND),
        left.reshape(ROWS, TB, TB), right.reshape(ROWS, TB, TB), near.reshape(ROWS, TB, TB), slot,
    )
    operands = [pltpu.with_memory_space_constraint(o, pltpu.HBM) for o in operands]
    results = pl.pallas_call(
        kernel,
        out_shape=(
            pltpu.VMEM(field, F32),
            pltpu.VMEM((COLS, BND), F32),
            pltpu.VMEM((COLS, CONDUCTORS), F32),
        ),
        in_specs=[hbm_spec] * len(operands),
        out_specs=(vmem_spec,) * 3,
        scratch_shapes=[
            pltpu.VMEM(field, F32),
            pltpu.VMEM((CX + 2, CY + 2, COLS, CZ), F32),
            pltpu.VMEM(field, F32),
            pltpu.VMEM((CX, CY * COLS, 2 * CZ), BF16),
            pltpu.VMEM((CX, CY, CZ), F32),
            pltpu.VMEM((CX, CY, CZ), F32),
            pltpu.VMEM((COLS, BND), F32),
            pltpu.VMEM((1, BND), jnp.int32),
            pltpu.SMEM((1, BND), jnp.int32),
            pltpu.VMEM((1, BND), jnp.int32),
            pltpu.SMEM((ROWS, TILES), jnp.int32),
            pltpu.VMEM((ROWS, TB, TB), BF16),
            pltpu.VMEM((ROWS, TB, TB), BF16),
            pltpu.VMEM((ROWS, TB, TB), BF16),
            pltpu.VMEM((GROUP, COLS, BND), F32),
            pltpu.VMEM((NZ, 1, BND), jnp.int32),
            pltpu.VMEM((CZ, 2 * BND), BF16),
            pltpu.VMEM((2 * CZ, 2 * CZ), BF16),
            pltpu.VMEM((2 * CZ, CZ), BF16),
            pltpu.VMEM((CY * COLS, 2 * CZ), BF16),
            pltpu.VMEM((NZ, COLS, BND), F32),
            pltpu.VMEM((NZ, 2 * COLS, BND), F32),
            pltpu.VMEM((NZ, 2 * COLS, BND), F32),
            pltpu.VMEM((COLS, BND), F32),
            pltpu.VMEM((PEERS, COLS, BND), F32),
            pltpu.VMEM((CY // 2, COLS, CZ), F32),
            pltpu.VMEM((CY // 2, COLS, CZ), F32),
            pltpu.VMEM((CY // 2, COLS, CZ), F32),
            pltpu.VMEM((COLS, BND), F32),
            dma((10,)), dma, dma((GROUP,)), dma, dma, dma, dma((8,)), dma((8,)),
            dma, dma, dma((2,)), dma((2,)), dma, dma,
        ],
        compiler_params=pltpu.CompilerParams(
            collective_id=0, has_side_effects=True, vmem_limit_bytes=40 * 1024 * 1024),
    )(*operands)
    out, bnd_out, charges = pl.pallas_call(
        deliver,
        out_shape=(
            pltpu.HBM((COLS, nodes, CZ), F32),
            pltpu.HBM((COLS, BND), F32),
            pltpu.HBM((COLS, CONDUCTORS), F32),
        ),
        in_specs=[vmem_spec] * 3,
        out_specs=(hbm_spec,) * 3,
        scratch_shapes=[dma, dma((2,))],
    )(*[pltpu.with_memory_space_constraint(r, pltpu.VMEM) for r in results])
    return out.reshape(vol.shape), bnd_out, charges.T


def solution(mesh):
    in_specs = (
        P(None, "gx", "gy", "gz"),
        P("gx", "gy", "gz"),
        P("gx", "gy", "gz"),
        P(None, ("gx", "gy", "gz")),
        P(("gx", "gy", "gz")),
        P(("gx", "gy", "gz")),
        P(("gx", "gy"), "gz", None, None),
        P(("gx", "gy"), "gz", None, None),
        P(("gx", "gy"), "gz", None, None),
        P(("gx", "gy"), "gz"),
    )
    out_specs = (P(None, "gx", "gy", "gz"), P(None, ("gx", "gy", "gz")), P())
    return jax.shard_map(shards, mesh=mesh, in_specs=in_specs, out_specs=out_specs, check_vma=False)
```

time: 45.4 us -> 26.5 us (0.58)
  local copies, waits for them, and re-layouts: 11.8 us -> 0 us
  Pallas kernels: 32.5 us -> 25.8 us
    unnamed x23 -> x0, local copies, waits for them, and re-layouts: 11.8 us -> none
    pallas_call x1 -> x2, Pallas kernels: 32.5 us -> 25.8 us  [the longest x1 24.4 us: shards(): pl.pallas_call(kernel, out_shape=(pltpu.VMEM(field, F32), pltpu.VMEM((COL...]
where the time goes in v2:
time: 26.5 us; the launch traced here: 26.4 us
  Pallas kernels  25.8 us (97%)
  between operations  0.64 us (2%)
    pallas_call x1, Pallas kernels, shards(): pl.pallas_call(kernel, out_shape=(pltpu.VMEM(field, F32), pltpu.VMEM((COL...  24.4 us
    pallas_call x1, Pallas kernels, shards(): pl.pallas_call(deliver, out_shape=(pltpu.HBM((COLS, nodes, CZ), F32), plt...  1.34 us

profile of v2, /device:TPU:1, one launch (start us, length us, event | category | flops | bytes accessed | tf_op | source)
XLA Modules:
  0.0 26.4 jit_solution(521108068801427698)
XLA Ops:
  0.6 24.4 %shard_map.121 = (f32[512,8,128]{2,1,0:T(8,128)S(1)}, f32[8,128]{1,0:T(8,128)S(1)}, f32[8,32]{1,0:T(8,128)S(1)}) custom-call(f32[8,512,128]{2,1,0:T(8,128)} %bitcast.8, f32[32,16,128]{2,1,0:T(8,128)} %scal.1, f32[32,16,128]{2,1,0:T(8,128)} %diag.1, f32[8,128]{1,0:T(8,128)} %bnd.1, s32[1,128]{1,0:T(1,128)} %bitcast.12, s32[1,128]{1,0:T(1,128)} %bitcast.13, ...), custom_call_target="tpu_custom_call" | custom-call | tf_op jit(solution)/shard_map/pallas_call | solution.py:424
  25.1 1.3 %shard_map.122 = (f32[8,512,128]{2,1,0:T(8,128)}, f32[8,128]{1,0:T(8,128)}, f32[8,32]{1,0:T(8,128)}) custom-call(f32[512,8,128]{2,1,0:T(8,128)S(1)} %get-tuple-element.9.field, f32[8,128]{1,0:T(8,128)S(1)} %get-tuple-element.10.rows, f32[8,32]{1,0:T(8,128)S(1)} %get-tuple-element.11.sums), custom_call_target="tpu_custom_call" | custom-call | tf_op jit(solution)/shard_map/pallas_call | solution.py:469

commit v3 on v2

--- a/solution.py
+++ b/solution.py
@@ -18,6 +18,10 @@
 CONDUCTORS = 32
 BND = 128
 GROUP = PEERS
+PLANE = [(3, 2), (2, 2), (3, 1), (3, 3), (2, 1), (2, 3), (1, 2), (0, 2), (3, 0), (2, 0), (1, 1), (1, 3), (0, 1), (0, 3), (1, 0)]
+LINE = [5, 4, 7, 3, 6, 2, 1]
+FIRST = [(3, 0), (2, 0), (3, 1), (2, 1), (1, 1), (0, 1), (1, 0)]
+SECOND = [(2, 2), (2, 1), (2, 3), (1, 2), (3, 2), (2, 0), (0, 2), (1, 1), (1, 3), (3, 1), (3, 3), (1, 0), (3, 0), (0, 1), (0, 3)]
 NEIGHBOURS = [(dx, dy) for dx in (-1, 0, 1) for dy in (-1, 0, 1) if (dx, dy) != (0, 0)]
 
 
@@ -37,6 +41,13 @@
 
 def dot_nt(a, b):
     return lax.dot_general(a, b, (((1,), (1,)), ((), ())), preferred_element_type=F32)
+
+
+def total_of(buf):
+    parts = [buf[i] for i in range(buf.shape[0])]
+    while len(parts) > 1:
+        parts = [a + b for a, b in zip(parts[::2], parts[1::2])]
+    return parts[0]
 
 
 def face(step, size):
@@ -186,7 +197,7 @@
     return lax.fori_loop(0, BND, trace_one, jnp.zeros((COLS, CZ), F32), unroll=8)
 
 
-def tile_products(xbuf, slots, rightb, leftb, nearb, pbuf):
+def tile_products(xbuf, slots, rightb, leftb, nearb):
     pieces = []
     for j in range(TILES):
         xj = jnp.concatenate([xbuf[2 * j], xbuf[2 * j + 1]], axis=1)
@@ -194,209 +205,201 @@
         pieces.append(jnp.concatenate([hi, lo], axis=0))
     xall = jnp.concatenate(pieces, axis=0).astype(BF16)
     lane2 = lax.broadcasted_iota(jnp.int32, (COLS, TB), 1)
+    parts = []
     for i in range(ROWS):
         proj = dot_nt(xall, rightb[i])
         acc = jnp.zeros((COLS, TB), F32)
         chosen = jnp.zeros((2 * COLS, TB), F32)
         for j in range(TILES):
-            is_far = slots[i, j] < 0
-            far = jnp.where(is_far, 1.0, 0.0).astype(F32)
+            far = jnp.where(slots[i, j] < 0, 1.0, 0.0).astype(F32)
             block = proj[16 * j:16 * j + 8] + proj[16 * j + 8:16 * j + 16]
             acc = jnp.where(lane2 // RANK == j, block * far, acc)
             chosen = chosen + pieces[j] * (1.0 - far)
         both = dot(stacked(acc), leftb[i]) + dot_nt(chosen.astype(BF16), nearb[i])
-        part = -(both[:COLS] + both[COLS:])
-        pbuf[2 * i] = part[:, :BND]
-        pbuf[2 * i + 1] = part[:, BND:]
-
-
-def conductor_sums(trbuf, labv, lbuf, pbuf, mbuf):
+        parts.append(-(both[:COLS] + both[COLS:]))
+    return jnp.concatenate(parts, axis=1)
+
+
+def members(labels):
     which = lax.broadcasted_iota(jnp.int32, (CONDUCTORS, BND), 0)
-
-    def members(labels):
-        return (which == labels).astype(F32).astype(BF16)
-
-    gathered = dot_nt(stacked(trbuf[...]), members(labv[...]))
-    for b in range(NZ):
-        gathered = gathered + dot_nt(stacked(pbuf[b]), members(lbuf[b]))
-    sums = jnp.concatenate([gathered[:COLS] + gathered[COLS:], jnp.zeros((COLS, BND - CONDUCTORS), F32)], axis=1)
-    for b in range(NZ):
-        mbuf[b, pl.ds(0, COLS), :] = pbuf[b]
-        mbuf[b, pl.ds(COLS, COLS), :] = sums
+    return (which == labels).astype(F32).astype(BF16)
+
+
+def conductor_sums(values, onehots):
+    both = dot_nt(stacked(values), onehots)
+    return both[:COLS] + both[COLS:]
 
 
 def kernel(
     vol, scal, diag, bnd, cell, lab, left, right, near, slot,
     obuf, bnd_out, charges,
     vbuf, wbuf, qbuf, lhs, sbuf, dbuf, bbuf, cellv, cells, labv, slots, leftb, rightb, nearb,
-    xbuf, lbuf, ohz, wz, ez, zc, pbuf, mbuf, rbuf, c1, c2, zsend, zlo, zhi, trbuf,
+    xbuf, lbuf, memb, ohz, wz, ez, zc, pbuf, rbuf, c1, c2, c3, c4, zsend, zlo, zhi, trbuf,
     load_sem, vol_sem, xs_sem, xr_sem, ls_sem, lr_sem, hs_sem, hr_sem,
-    ms_sem, mr_sem, zs_sem, zr_sem, cs_sem, cr_sem,
+    ms_sem, mr_sem, zs_sem, zr_sem, cs_sem, cr_sem, ds_sem, dr_sem,
 ):
     gx, gy, gz = lax.axis_index("gx"), lax.axis_index("gy"), lax.axis_index("gz")
-    me2 = gx * NY + gy
-    group = me2 // 2
+    group = (gx * NY + gy) // 2
     pos = lax.rem(gy, 2) * NZ + gz
+    own_group = group == gz
     lane = lax.broadcasted_iota(jnp.int32, (COLS, CZ), 1)
+
+    def remote(src, dst, send_sem, recv_sem, device):
+        return pltpu.make_async_remote_copy(src, dst, send_sem, recv_sem, device_id=device, device_id_type=MESH)
+
+    def plane(a, b):
+        return jnp.bitwise_xor(gx, a), lax.rem(gy + b, NY)
+
+    def line(k):
+        return gx, gy, jnp.bitwise_xor(gz, k)
+
+    first = [(jnp.bitwise_xor(gx, a), gy, jnp.bitwise_xor(gz, b)) for a, b in FIRST]
+    second = [(jnp.bitwise_xor(gx, 1), lax.rem(gy + b, NY), jnp.bitwise_xor(gz, 2 * c)) for b, c in SECOND]
 
     small = [(bnd, bbuf), (lab, labv), (cell, cells), (cell, cellv), (slot, slots),
              (scal, sbuf), (diag, dbuf), (right, rightb), (left, leftb), (near, nearb)]
     loads = [pltpu.make_async_copy(s, d, load_sem.at[i]) for i, (s, d) in enumerate(small)]
     (l_bnd, l_lab, l_cells, l_cellv, l_slot, l_scal, l_diag, l_right, l_left, l_near) = loads
-    for l in (l_bnd, l_lab, l_scal):
-        l.start()
-    for c in range(COLS):
-        pltpu.make_async_copy(vol.at[c], vbuf.at[:, c, :], vol_sem).start()
-    for l in (l_cells, l_cellv, l_slot, l_right, l_left, l_near, l_diag):
-        l.start()
-
-    zero = jnp.zeros((COLS, CZ), F32)
+    l_bnd.start()
+    l_lab.start()
+
     for x in (0, CX + 1):
         wbuf[x] = jnp.zeros((CY + 2, COLS, CZ), F32)
     for y in (0, CY + 1):
         wbuf[:, y] = jnp.zeros((CX + 2, COLS, CZ), F32)
     zlo[...] = jnp.zeros_like(zlo)
     zhi[...] = jnp.zeros_like(zhi)
-    zsend[...] = jnp.zeros_like(zsend)
 
     barrier = pltpu.get_barrier_semaphore()
-    own_group = group == gz
 
     def greet(device):
         pl.semaphore_signal(barrier, inc=1, device_id=device, device_id_type=MESH)
 
-    for p in range(GROUP):
-        source = (gz // 2, lax.rem(gz, 2) * 2 + p // NZ, p % NZ)
-        pl.when(jnp.logical_not(jnp.logical_and(own_group, pos == p)))(functools.partial(greet, source))
-    for d in range(1, NZ):
-        greet((gx, gy, lax.rem(gz + d, NZ)))
-    for e in range(1, PEERS):
-        other = lax.rem(me2 + e, PEERS)
-        greet((other // NY, lax.rem(other, NY), gz))
-    own = own_group.astype(jnp.int32)
-
+    for k in LINE + [0]:
+        for p in range(2):
+            source = (gz // 2, lax.rem(gz, 2) * 2 + p, jnp.bitwise_xor(gz, k))
+            if k:
+                greet(source)
+            else:
+                here = jnp.logical_and(own_group, lax.rem(gy, 2) == p)
+                pl.when(jnp.logical_not(here))(functools.partial(greet, source))
+    for device in second:
+        greet(device)
+    for k in LINE:
+        greet(line(k))
+    for device in first:
+        greet(device)
+
+    def within(a, b):
+        return jnp.logical_and(jnp.logical_and(a >= 0, a < NX), jnp.logical_and(b >= 0, b < NY))
+
+    halo = []
+    count = GROUP - own_group.astype(jnp.int32) + len(SECOND) + len(LINE) + len(FIRST)
+    for i, (dx, dy) in enumerate(NEIGHBOURS):
+        (fx, tx), (fy, ty) = face(dx, CX), face(dy, CY)
+        device = (lax.rem(gx + dx + NX, NX), lax.rem(gy + dy + NY, NY), gz)
+        to, come = within(gx + dx, gy + dy), within(gx - dx, gy - dy)
+        halo.append((remote(wbuf.at[fx, fy], wbuf.at[tx, ty], hs_sem.at[i], hr_sem.at[i], device), to, come))
+        pl.when(to)(functools.partial(greet, device))
+        count = count + come.astype(jnp.int32)
+
+    l_scal.start()
+    for c in range(COLS):
+        pltpu.make_async_copy(vol.at[c], vbuf.at[:, c, :], vol_sem).start()
+    for l in (l_cells, l_cellv, l_diag, l_slot, l_right, l_left, l_near):
+        l.start()
     l_bnd.wait()
     l_lab.wait()
-    pl.semaphore_wait(barrier, GROUP - own + (NZ - 1) + (PEERS - 1))
-
-    def x_copy(t):
-        return pltpu.make_async_remote_copy(
-            bbuf, xbuf.at[pos], xs_sem.at[t], xr_sem,
-            device_id=(t // NY, t % NY, group), device_id_type=MESH)
-
+    pl.semaphore_wait(barrier, count)
+
+    x_sends = [remote(bbuf, xbuf.at[pos], xs_sem.at[i], xr_sem, (*plane(a, b), group)) for i, (a, b) in enumerate(PLANE)]
+    x_last = remote(bbuf, xbuf.at[pos], xs_sem.at[len(PLANE)], xr_sem, (gx, gy, group))
     x_self = pltpu.make_async_copy(bbuf, xbuf.at[pos], xr_sem)
-    for t in range(GROUP):
-        mine = jnp.logical_and(own_group, me2 == t)
-        pl.when(jnp.logical_not(mine))(lambda t=t: x_copy(t).start())
-    pl.when(own_group)(lambda: x_self.start())
-    lbuf[gz] = labv[...]
-    label_sends = [
-        pltpu.make_async_remote_copy(
-            labv, lbuf.at[gz], ls_sem, lr_sem,
-            device_id=(gx, gy, lax.rem(gz + d, NZ)), device_id_type=MESH)
-        for d in range(1, NZ)]
+    for s in x_sends:
+        s.start()
+    pl.when(jnp.logical_not(own_group))(x_last.start)
+    pl.when(own_group)(x_self.start)
+    label_sends = [remote(labv, lbuf.at[gz], ls_sem, lr_sem, line(k)) for k in LINE]
     for s in label_sends:
         s.start()
+    lbuf[gz] = labv[...]
 
     l_scal.wait()
     pltpu.make_async_copy(vbuf, vbuf, vol_sem).wait()
-
     scale_pass(sbuf, vbuf, wbuf)
-
-    halo = []
-    for i, (dx, dy) in enumerate(NEIGHBOURS):
-        (fx, tx), (fy, ty) = face(dx, CX), face(dy, CY)
-        copy = pltpu.make_async_remote_copy(
-            wbuf.at[fx, fy], wbuf.at[tx, ty], hs_sem.at[i], hr_sem.at[i],
-            device_id=(lax.rem(gx + dx + NX, NX), lax.rem(gy + dy + NY, NY), gz), device_id_type=MESH)
-
-        def within(a, b):
-            return jnp.logical_and(jnp.logical_and(a >= 0, a < NX), jnp.logical_and(b >= 0, b < NY))
-
-        to, come = within(gx + dx, gy + dy), within(gx - dx, gy - dy)
+    for copy, to, come in halo:
         pl.when(to)(copy.start)
-        halo.append((copy, to, come))
 
     l_cells.wait()
     l_cellv.wait()
-
+    l_diag.wait()
     trbuf[...] = trace_nodes(cells, vbuf, lane)
     line_weights(wz, ez)
     node_columns(cellv, ohz)
-    l_diag.wait()
     node_pass(bbuf, cellv, ohz, vbuf, dbuf, lhs, obuf)
+    zsend[...] = jnp.zeros_like(zsend)
+    c1[...] = jnp.zeros_like(c1)
+    own_sums = conductor_sums(trbuf[...], members(labv[...]))
+
+    pltpu.make_async_copy(lbuf.at[pl.ds(0, NZ - 1)], lbuf.at[pl.ds(0, NZ - 1)], lr_sem).wait()
+    for b in range(NZ):
+        memb[:, pl.ds(b * BND, BND)] = members(lbuf[b])
 
     l_slot.wait()
     l_right.wait()
     l_left.wait()
     l_near.wait()
     pltpu.make_async_copy(xbuf, xbuf, xr_sem).wait()
-    tile_products(xbuf, slots, rightb, leftb, nearb, pbuf)
-    pltpu.make_async_copy(lbuf.at[pl.ds(0, NZ - 1)], lbuf.at[pl.ds(0, NZ - 1)], lr_sem).wait()
-    conductor_sums(trbuf, labv, lbuf, pbuf, mbuf)
-
-    row_sends = []
-    for d in range(1, NZ):
-        other = lax.rem(gz + d, NZ)
-        row_sends.append(pltpu.make_async_remote_copy(
-            mbuf.at[other], rbuf.at[gz], ms_sem, mr_sem,
-            device_id=(gx, gy, other), device_id_type=MESH))
+    values = tile_products(xbuf, slots, rightb, leftb, nearb)
+    c1[:, pl.ds(0, CONDUCTORS)] = own_sums + conductor_sums(values, memb[...])
+    place = gx * 2 + lax.rem(gz, 2)
+    first_sends = [remote(c1, c2.at[place], cs_sem, cr_sem, device) for device in first]
+    for s in first_sends:
+        s.start()
+    c2[place] = c1[...]
+
+    for b in range(NZ):
+        pbuf[b] = values[:, b * BND:(b + 1) * BND]
+    row_sends = [remote(pbuf.at[jnp.bitwise_xor(gz, k)], rbuf.at[gz], ms_sem, mr_sem, line(k)) for k in LINE]
     for s in row_sends:
         s.start()
-    rbuf[gz] = mbuf[gz]
+    rbuf[gz] = pbuf[gz]
 
     for copy, to, come in halo:
         pl.when(come)(copy.wait_recv)
-
     line_pass(wbuf, lhs, qbuf)
     sum_pass(lhs, wz, qbuf, sbuf, obuf, zsend, lane)
-
     up, down = gz + 1 < NZ, gz > 0
-    z_up = pltpu.make_async_remote_copy(
-        zsend, zlo, zs_sem.at[0], zr_sem.at[0],
-        device_id=(gx, gy, lax.rem(gz + 1, NZ)), device_id_type=MESH)
-    z_down = pltpu.make_async_remote_copy(
-        zsend, zhi, zs_sem.at[1], zr_sem.at[1],
-        device_id=(gx, gy, lax.rem(gz + NZ - 1, NZ)), device_id_type=MESH)
+    z_up = remote(zsend, zlo, zs_sem.at[0], zr_sem.at[0], (gx, gy, lax.rem(gz + 1, NZ)))
+    z_down = remote(zsend, zhi, zs_sem.at[1], zr_sem.at[1], (gx, gy, lax.rem(gz + NZ - 1, NZ)))
     pl.when(up)(z_up.start)
     pl.when(down)(z_down.start)
 
+    pltpu.make_async_copy(c2.at[pl.ds(0, len(FIRST))], c2.at[pl.ds(0, len(FIRST))], cr_sem).wait()
+    c3[...] = total_of(c2)
+    place = gy * 4 + gz // 2
+    second_sends = [remote(c3, c4.at[place], ds_sem, dr_sem, device) for device in second]
+    for s in second_sends:
+        s.start()
+    c4[place] = c3[...]
+
     pltpu.make_async_copy(rbuf.at[pl.ds(0, NZ - 1)], rbuf.at[pl.ds(0, NZ - 1)], mr_sem).wait()
-    total = rbuf[0]
-    for b in range(1, NZ):
-        total = total + rbuf[b]
-    bnd_out[...] = trbuf[...] + total[:COLS]
-    c1[...] = total[COLS:]
-    c_sends = []
-    for e in range(1, PEERS):
-        other = lax.rem(me2 + e, PEERS)
-        c_sends.append(pltpu.make_async_remote_copy(
-            c1, c2.at[me2], cs_sem, cr_sem,
-            device_id=(other // NY, lax.rem(other, NY), gz), device_id_type=MESH))
-    for s in c_sends:
-        s.start()
-    c2[me2] = c1[...]
-
+    bnd_out[...] = trbuf[...] + total_of(rbuf)
     pl.when(down)(z_up.wait_recv)
     pl.when(up)(z_down.wait_recv)
     end_rows(zlo, zhi, zc, lane)
     end_pass(0, CX, zc, ez, sbuf, obuf)
 
-    pltpu.make_async_copy(c2.at[pl.ds(0, PEERS - 1)], c2.at[pl.ds(0, PEERS - 1)], cr_sem).wait()
-    total = c2[0]
-    for b in range(1, PEERS):
-        total = total + c2[b]
-    charges[...] = total[:, :CONDUCTORS] * (CONDUCTORS / (BND * NX * NY * NZ)) ** 0.5
-
-    for t in range(GROUP):
-        mine = jnp.logical_and(own_group, me2 == t)
-        pl.when(jnp.logical_not(mine))(lambda t=t: x_copy(t).wait_send())
-    for s in label_sends + row_sends + c_sends:
+    for s in x_sends + label_sends + first_sends + row_sends + second_sends:
         s.wait_send()
+    pl.when(jnp.logical_not(own_group))(x_last.wait_send)
     for copy, to, come in halo:
         pl.when(to)(copy.wait_send)
     pl.when(up)(z_up.wait_send)
     pl.when(down)(z_down.wait_send)
+
+    pltpu.make_async_copy(c4.at[pl.ds(0, len(SECOND))], c4.at[pl.ds(0, len(SECOND))], dr_sem).wait()
+    charges[...] = total_of(c4)[:, :CONDUCTORS] * (CONDUCTORS / (BND * NX * NY * NZ)) ** 0.5
 
 
 def deliver(field, rows, sums, out, bnd_out, charges, sem, small_sem):
@@ -447,21 +450,23 @@
             pltpu.VMEM((ROWS, TB, TB), BF16),
             pltpu.VMEM((GROUP, COLS, BND), F32),
             pltpu.VMEM((NZ, 1, BND), jnp.int32),
+            pltpu.VMEM((CONDUCTORS, NZ * BND), BF16),
             pltpu.VMEM((CZ, 2 * BND), BF16),
             pltpu.VMEM((2 * CZ, 2 * CZ), BF16),
             pltpu.VMEM((2 * CZ, CZ), BF16),
             pltpu.VMEM((CY * COLS, 2 * CZ), BF16),
             pltpu.VMEM((NZ, COLS, BND), F32),
-            pltpu.VMEM((NZ, 2 * COLS, BND), F32),
-            pltpu.VMEM((NZ, 2 * COLS, BND), F32),
+            pltpu.VMEM((NZ, COLS, BND), F32),
             pltpu.VMEM((COLS, BND), F32),
-            pltpu.VMEM((PEERS, COLS, BND), F32),
+            pltpu.VMEM((len(FIRST) + 1, COLS, BND), F32),
+            pltpu.VMEM((COLS, BND), F32),
+            pltpu.VMEM((len(SECOND) + 1, COLS, BND), F32),
             pltpu.VMEM((CY // 2, COLS, CZ), F32),
             pltpu.VMEM((CY // 2, COLS, CZ), F32),
             pltpu.VMEM((CY // 2, COLS, CZ), F32),
             pltpu.VMEM((COLS, BND), F32),
             dma((10,)), dma, dma((GROUP,)), dma, dma, dma, dma((8,)), dma((8,)),
-            dma, dma, dma((2,)), dma((2,)), dma, dma,
+            dma, dma, dma((2,)), dma((2,)), dma, dma, dma, dma,
         ],
         compiler_params=pltpu.CompilerParams(
             collective_id=0, has_side_effects=True, vmem_limit_bytes=40 * 1024 * 1024),

time: 26.5 us -> 25.8 us (0.974)
  Pallas kernels: 25.8 us -> 25 us
    pallas_call x1, Pallas kernels: 24.4 us -> 23.7 us  [shards(): pl.pallas_call(kernel, out_shape=(pltpu.VMEM(field, F32), pltpu.VMEM((COL...]
where the time goes in v3:
time: 25.8 us; the launch traced here: 25.7 us
  Pallas kernels  25 us (97%)
  between operations  0.64 us (2%)
    pallas_call x1, Pallas kernels, shards(): pl.pallas_call(kernel, out_shape=(pltpu.VMEM(field, F32), pltpu.VMEM((COL...  23.7 us
    pallas_call x1, Pallas kernels, shards(): pl.pallas_call(deliver, out_shape=(pltpu.HBM((COLS, nodes, CZ), F32), plt...  1.34 us

profile of v3, /device:TPU:1, one launch (start us, length us, event | category | flops | bytes accessed | tf_op | source)
XLA Modules:
  0.0 25.7 jit_solution(9134244700619496836)
XLA Ops:
  0.6 23.7 %shard_map.121 = (f32[512,8,128]{2,1,0:T(8,128)S(1)}, f32[8,128]{1,0:T(8,128)S(1)}, f32[8,32]{1,0:T(8,128)S(1)}) custom-call(f32[8,512,128]{2,1,0:T(8,128)} %bitcast.8, f32[32,16,128]{2,1,0:T(8,128)} %scal.1, f32[32,16,128]{2,1,0:T(8,128)} %diag.1, f32[8,128]{1,0:T(8,128)} %bnd.1, s32[1,128]{1,0:T(1,128)} %bitcast.12, s32[1,128]{1,0:T(1,128)} %bitcast.13, ...), custom_call_target="tpu_custom_call" | custom-call | tf_op jit(solution)/shard_map/pallas_call | solution.py:427
  24.3 1.3 %shard_map.122 = (f32[8,512,128]{2,1,0:T(8,128)}, f32[8,128]{1,0:T(8,128)}, f32[8,32]{1,0:T(8,128)}) custom-call(f32[512,8,128]{2,1,0:T(8,128)S(1)} %get-tuple-element.9.field, f32[8,128]{1,0:T(8,128)S(1)} %get-tuple-element.10.rows, f32[8,32]{1,0:T(8,128)S(1)} %get-tuple-element.11.sums), custom_call_target="tpu_custom_call" | custom-call | tf_op jit(solution)/shard_map/pallas_call | solution.py:474

commit v4 on v3

--- a/solution.py
+++ b/solution.py
@@ -22,6 +22,7 @@
 LINE = [5, 4, 7, 3, 6, 2, 1]
 FIRST = [(3, 0), (2, 0), (3, 1), (2, 1), (1, 1), (0, 1), (1, 0)]
 SECOND = [(2, 2), (2, 1), (2, 3), (1, 2), (3, 2), (2, 0), (0, 2), (1, 1), (1, 3), (3, 1), (3, 3), (1, 0), (3, 0), (0, 1), (0, 3)]
+HEAD = (1, 0, 0)
 NEIGHBOURS = [(dx, dy) for dx in (-1, 0, 1) for dy in (-1, 0, 1) if (dx, dy) != (0, 0)]
 
 
@@ -230,13 +231,41 @@
     return both[:COLS] + both[COLS:]
 
 
+def conductor_weights(memb, slots, rightb, leftb, nearb, farl, nearl, wcon):
+    lane = lax.broadcasted_iota(jnp.int32, (CONDUCTORS, TB), 1) // RANK
+    side = CONDUCTORS * TILES
+    for i in range(ROWS):
+        cols = pl.ds(TB * i, TB)
+        rows = memb[:, cols]
+        pieces = [p.astype(BF16) for p in split(dot_nt(rows, leftb[i]))]
+        for j in range(TILES):
+            far = jnp.where(slots[i, j] < 0, 1.0, 0.0).astype(F32)
+            mask = jnp.where(lane == j, far, 0.0).astype(BF16)
+            for p in range(2):
+                farl[pl.ds(side * p + CONDUCTORS * j, CONDUCTORS), cols] = pieces[p] * mask
+            nearl[pl.ds(CONDUCTORS * j, CONDUCTORS), cols] = rows * jnp.full((CONDUCTORS, TB), 1.0 - far).astype(BF16)
+    both = dot(farl[...], rightb[...].reshape(ROWS * TB, TB))
+    total = both[:side] + both[side:] + dot(nearl[...], nearb[...].reshape(ROWS * TB, TB))
+    for p, piece in enumerate(split(total)):
+        wcon[pl.ds(side * p, side), :] = piece.astype(BF16)
+
+
+def conductor_products(xbuf, wcon):
+    total = jnp.zeros((2 * COLS, CONDUCTORS), F32)
+    for j in range(TILES):
+        xj = stacked(jnp.concatenate([xbuf[2 * j], xbuf[2 * j + 1]], axis=1))
+        for p in range(2):
+            total = total + dot_nt(xj, wcon[pl.ds(CONDUCTORS * (TILES * p + j), CONDUCTORS), :])
+    return total[:COLS] + total[COLS:]
+
+
 def kernel(
     vol, scal, diag, bnd, cell, lab, left, right, near, slot,
     obuf, bnd_out, charges,
     vbuf, wbuf, qbuf, lhs, sbuf, dbuf, bbuf, cellv, cells, labv, slots, leftb, rightb, nearb,
-    xbuf, lbuf, memb, ohz, wz, ez, zc, pbuf, rbuf, c1, c2, c3, c4, zsend, zlo, zhi, trbuf,
+    xbuf, lbuf, memb, farl, nearl, wcon, ohz, wz, ez, zc, pbuf, rbuf, c1, c2, c3, c4, d1, zsend, zlo, zhi, trbuf,
     load_sem, vol_sem, xs_sem, xr_sem, ls_sem, lr_sem, hs_sem, hr_sem,
-    ms_sem, mr_sem, zs_sem, zr_sem, cs_sem, cr_sem, ds_sem, dr_sem,
+    ms_sem, mr_sem, zs_sem, zr_sem, cs_sem, cr_sem, ds_sem, dr_sem, hd_sem, hd_sem2,
 ):
     gx, gy, gz = lax.axis_index("gx"), lax.axis_index("gy"), lax.axis_index("gz")
     group = (gx * NY + gy) // 2
@@ -253,6 +282,8 @@
     def line(k):
         return gx, gy, jnp.bitwise_xor(gz, k)
 
+    at_head = jnp.logical_and(gx == HEAD[0], jnp.logical_and(gy == HEAD[1], gz == HEAD[2]))
+    away = jnp.logical_not(at_head)
     first = [(jnp.bitwise_xor(gx, a), gy, jnp.bitwise_xor(gz, b)) for a, b in FIRST]
     second = [(jnp.bitwise_xor(gx, 1), lax.rem(gy + b, NY), jnp.bitwise_xor(gz, 2 * c)) for b, c in SECOND]
 
@@ -303,6 +334,15 @@
         pl.when(to)(functools.partial(greet, device))
         count = count + come.astype(jnp.int32)
 
+    @pl.when(at_head)
+    def _():
+        @pl.loop(0, NX * NY * NZ)
+        def _(i):
+            device = (i // (NY * NZ), lax.rem(i // NZ, NY), lax.rem(i, NZ))
+            pl.when(i != (HEAD[0] * NY + HEAD[1]) * NZ + HEAD[2])(lambda: greet(device))
+
+    count = count + away.astype(jnp.int32)
+
     l_scal.start()
     for c in range(COLS):
         pltpu.make_async_copy(vol.at[c], vbuf.at[:, c, :], vol_sem).start()
@@ -315,13 +355,11 @@
     x_sends = [remote(bbuf, xbuf.at[pos], xs_sem.at[i], xr_sem, (*plane(a, b), group)) for i, (a, b) in enumerate(PLANE)]
     x_last = remote(bbuf, xbuf.at[pos], xs_sem.at[len(PLANE)], xr_sem, (gx, gy, group))
     x_self = pltpu.make_async_copy(bbuf, xbuf.at[pos], xr_sem)
-    for s in x_sends:
+    label_sends = [remote(labv, lbuf.at[gz], ls_sem, lr_sem, line(k)) for k in LINE]
+    for s in x_sends[:2] + label_sends + x_sends[2:]:
         s.start()
     pl.when(jnp.logical_not(own_group))(x_last.start)
     pl.when(own_group)(x_self.start)
-    label_sends = [remote(labv, lbuf.at[gz], ls_sem, lr_sem, line(k)) for k in LINE]
-    for s in label_sends:
-        s.start()
     lbuf[gz] = labv[...]
 
     l_scal.wait()
@@ -349,15 +387,20 @@
     l_right.wait()
     l_left.wait()
     l_near.wait()
+    conductor_weights(memb, slots, rightb, leftb, nearb, farl, nearl, wcon)
+
     pltpu.make_async_copy(xbuf, xbuf, xr_sem).wait()
-    values = tile_products(xbuf, slots, rightb, leftb, nearb)
-    c1[:, pl.ds(0, CONDUCTORS)] = own_sums + conductor_sums(values, memb[...])
+    c1[:, pl.ds(0, CONDUCTORS)] = own_sums - conductor_products(xbuf, wcon)
     place = gx * 2 + lax.rem(gz, 2)
+    head_place = gy * 4 + gz // 2
+    head_send = remote(c1, d1.at[head_place, place], hd_sem, hd_sem2, HEAD)
+    pl.when(away)(head_send.start)
     first_sends = [remote(c1, c2.at[place], cs_sem, cr_sem, device) for device in first]
     for s in first_sends:
         s.start()
     c2[place] = c1[...]
 
+    values = tile_products(xbuf, slots, rightb, leftb, nearb)
     for b in range(NZ):
         pbuf[b] = values[:, b * BND:(b + 1) * BND]
     row_sends = [remote(pbuf.at[jnp.bitwise_xor(gz, k)], rbuf.at[gz], ms_sem, mr_sem, line(k)) for k in LINE]
@@ -378,9 +421,13 @@
     pltpu.make_async_copy(c2.at[pl.ds(0, len(FIRST))], c2.at[pl.ds(0, len(FIRST))], cr_sem).wait()
     c3[...] = total_of(c2)
     place = gy * 4 + gz // 2
-    second_sends = [remote(c3, c4.at[place], ds_sem, dr_sem, device) for device in second]
-    for s in second_sends:
-        s.start()
+    second_sends = []
+    for i, (device, (b, c)) in enumerate(zip(second, SECOND)):
+        to_head = jnp.logical_and(
+            jnp.logical_and(gx == HEAD[0] ^ 1, gy == (HEAD[1] - b) % NY), gz == HEAD[2] ^ (2 * c))
+        second_sends.append((remote(c3, c4.at[place], ds_sem.at[i], dr_sem, device), jnp.logical_not(to_head)))
+    for s, to in second_sends:
+        pl.when(to)(s.start)
     c4[place] = c3[...]
 
     pltpu.make_async_copy(rbuf.at[pl.ds(0, NZ - 1)], rbuf.at[pl.ds(0, NZ - 1)], mr_sem).wait()
@@ -390,16 +437,32 @@
     end_rows(zlo, zhi, zc, lane)
     end_pass(0, CX, zc, ez, sbuf, obuf)
 
-    for s in x_sends + label_sends + first_sends + row_sends + second_sends:
+    for s in x_sends + label_sends + first_sends + row_sends:
         s.wait_send()
+    for s, to in second_sends:
+        pl.when(to)(s.wait_send)
+    pl.when(away)(head_send.wait_send)
     pl.when(jnp.logical_not(own_group))(x_last.wait_send)
     for copy, to, come in halo:
         pl.when(to)(copy.wait_send)
     pl.when(up)(z_up.wait_send)
     pl.when(down)(z_down.wait_send)
 
-    pltpu.make_async_copy(c4.at[pl.ds(0, len(SECOND))], c4.at[pl.ds(0, len(SECOND))], dr_sem).wait()
-    charges[...] = total_of(c4)[:, :CONDUCTORS] * (CONDUCTORS / (BND * NX * NY * NZ)) ** 0.5
+    scale = (CONDUCTORS / (BND * NX * NY * NZ)) ** 0.5
+
+    @pl.when(away)
+    def _():
+        pltpu.make_async_copy(c4.at[pl.ds(0, len(SECOND))], c4.at[pl.ds(0, len(SECOND))], dr_sem).wait()
+        charges[...] = total_of(c4)[:, :CONDUCTORS] * scale
+
+    @pl.when(at_head)
+    def _():
+        d1[HEAD[1] * 4 + HEAD[2] // 2, HEAD[0] * 2 + HEAD[2] % 2] = c1[...]
+        rest = d1.reshape(NX * NY * NZ, COLS, BND).at[pl.ds(0, NX * NY * NZ - 1)]
+        pltpu.make_async_copy(rest, rest, hd_sem2).wait()
+        for k in range(len(SECOND) + 1):
+            c4[k] = total_of(d1.at[k])
+        charges[...] = total_of(c4)[:, :CONDUCTORS] * scale
 
 
 def deliver(field, rows, sums, out, bnd_out, charges, sem, small_sem):
@@ -451,6 +514,9 @@
             pltpu.VMEM((GROUP, COLS, BND), F32),
             pltpu.VMEM((NZ, 1, BND), jnp.int32),
             pltpu.VMEM((CONDUCTORS, NZ * BND), BF16),
+            pltpu.VMEM((2 * CONDUCTORS * TILES, ROWS * TB), BF16),
+            pltpu.VMEM((CONDUCTORS * TILES, ROWS * TB), BF16),
+            pltpu.VMEM((2 * CONDUCTORS * TILES, TB), BF16),
             pltpu.VMEM((CZ, 2 * BND), BF16),
             pltpu.VMEM((2 * CZ, 2 * CZ), BF16),
             pltpu.VMEM((2 * CZ, CZ), BF16),
@@ -461,12 +527,13 @@
             pltpu.VMEM((len(FIRST) + 1, COLS, BND), F32),
             pltpu.VMEM((COLS, BND), F32),
             pltpu.VMEM((len(SECOND) + 1, COLS, BND), F32),
+            pltpu.VMEM((len(SECOND) + 1, len(FIRST) + 1, COLS, BND), F32),
             pltpu.VMEM((CY // 2, COLS, CZ), F32),
             pltpu.VMEM((CY // 2, COLS, CZ), F32),
             pltpu.VMEM((CY // 2, COLS, CZ), F32),
             pltpu.VMEM((COLS, BND), F32),
             dma((10,)), dma, dma((GROUP,)), dma, dma, dma, dma((8,)), dma((8,)),
-            dma, dma, dma((2,)), dma((2,)), dma, dma, dma, dma,
+            dma, dma, dma((2,)), dma((2,)), dma, dma, dma((len(SECOND),)), dma, dma, dma,
         ],
         compiler_params=pltpu.CompilerParams(
             collective_id=0, has_side_effects=True, vmem_limit_bytes=40 * 1024 * 1024),

time: 25.8 us -> 24.2 us (0.938); the launches traced: 25.7 us -> 23.8 us
  Pallas kernels: 25 us -> 23.1 us
    pallas_call x1, Pallas kernels: 23.7 us -> 21.8 us  [shards(): pl.pallas_call(kernel, out_shape=(pltpu.VMEM(field, F32), pltpu.VMEM((COL...]
where the time goes in v4:
time: 24.2 us; the launch traced here: 23.8 us
  Pallas kernels  23.1 us (95%)
  between operations  0.64 us (3%)
    pallas_call x1, Pallas kernels, shards(): pl.pallas_call(kernel, out_shape=(pltpu.VMEM(field, F32), pltpu.VMEM((COL...  21.8 us
    pallas_call x1, Pallas kernels, shards(): pl.pallas_call(deliver, out_shape=(pltpu.HBM((COLS, nodes, CZ), F32), plt...  1.34 us

profile of v4, /device:TPU:1, one launch (start us, length us, event | category | flops | bytes accessed | tf_op | source)
XLA Modules:
  0.0 23.8 jit_solution(18131920569289280988)
XLA Ops:
  0.6 21.8 %shard_map.121 = (f32[512,8,128]{2,1,0:T(8,128)S(1)}, f32[8,128]{1,0:T(8,128)S(1)}, f32[8,32]{1,0:T(8,128)S(1)}) custom-call(f32[8,512,128]{2,1,0:T(8,128)} %bitcast.8, f32[32,16,128]{2,1,0:T(8,128)} %scal.1, f32[32,16,128]{2,1,0:T(8,128)} %diag.1, f32[8,128]{1,0:T(8,128)} %bnd.1, s32[1,128]{1,0:T(1,128)} %bitcast.12, s32[1,128]{1,0:T(1,128)} %bitcast.13, ...), custom_call_target="tpu_custom_call" | custom-call | tf_op jit(solution)/shard_map/pallas_call | solution.py:490
  22.4 1.3 %shard_map.122 = (f32[8,512,128]{2,1,0:T(8,128)}, f32[8,128]{1,0:T(8,128)}, f32[8,32]{1,0:T(8,128)}) custom-call(f32[512,8,128]{2,1,0:T(8,128)S(1)} %get-tuple-element.9.field, f32[8,128]{1,0:T(8,128)S(1)} %get-tuple-element.10.rows, f32[8,32]{1,0:T(8,128)S(1)} %get-tuple-element.11.sums), custom_call_target="tpu_custom_call" | custom-call | tf_op jit(solution)/shard_map/pallas_call | solution.py:541

commit v5 on v4

--- a/solution.py
+++ b/solution.py
@@ -106,8 +106,7 @@
                 both = jnp.concatenate([jnp.where(h, pieces[p], 0.0) for h in here], axis=0)
                 lhs[x, pl.ds(COLS * y, 2 * COLS), pl.ds(p * BND, BND)] = both.astype(BF16)
 
-    @pl.loop(0, CX // GX)
-    def _(g):
+    for g in range(CX // GX):
         extra = dot_nt(lhs[pl.ds(g * GX, GX)].reshape(GX * CY * COLS, 2 * BND), ohz[...])
         for i in range(GX):
             for y in range(CY):
@@ -138,8 +137,7 @@
     spot = jnp.bitwise_and(lane, CX - 1)
     half = lax.shift_right_logical(lane, 6)
 
-    @pl.loop(0, CX // GX)
-    def _(g):
+    for g in range(CX // GX):
         r = dot(lhs[pl.ds(g * GX, GX)].reshape(GX * CY * COLS, 2 * CZ), wz[...])
         ends = [zsend[y] for y in range(CY // 2)]
         for i in range(GX):
@@ -169,11 +167,10 @@
         zc[pl.ds(COLS * y, 2 * COLS), pl.ds(CZ, CZ)] = (z - hi.astype(F32)).astype(BF16)
 
 
-def end_pass(k, chunk, zc, ez, sbuf, obuf):
+def end_pass(zc, ez, sbuf, obuf):
     lane2 = jnp.bitwise_and(lax.broadcasted_iota(jnp.int32, (2 * COLS, 2 * CZ), 1), CX - 1)
 
-    @pl.loop(k * (chunk // GX), (k + 1) * (chunk // GX))
-    def _(g):
+    for g in range(CX // GX):
         rows = []
         for i in range(GX):
             here = (lane2 == g * GX + i).astype(F32).astype(BF16)
@@ -435,7 +432,7 @@
     pl.when(down)(z_up.wait_recv)
     pl.when(up)(z_down.wait_recv)
     end_rows(zlo, zhi, zc, lane)
-    end_pass(0, CX, zc, ez, sbuf, obuf)
+    end_pass(zc, ez, sbuf, obuf)
 
     for s in x_sends + label_sends + first_sends + row_sends:
         s.wait_send()

time: 24.2 us -> 23.9 us (0.988)
  the two profiles are of different devices: /device:TPU:1 before, /device:TPU:0 now
where the time goes in v5:
time: 23.9 us; the launch traced here: 23.7 us
  Pallas kernels  23.1 us (97%)
  between operations  0.64 us (3%)
    pallas_call x1, Pallas kernels, shards(): pl.pallas_call(kernel, out_shape=(pltpu.VMEM(field, F32), pltpu.VMEM((COL...  21.8 us
    pallas_call x1, Pallas kernels, shards(): pl.pallas_call(deliver, out_shape=(pltpu.HBM((COLS, nodes, CZ), F32), plt...  1.34 us

profile of v5, /device:TPU:0, one launch (start us, length us, event | category | flops | bytes accessed | tf_op | source)
XLA Modules:
  0.0 23.7 jit_solution(15830461753825658191)
XLA Ops:
  0.6 21.8 %shard_map.121 = (f32[512,8,128]{2,1,0:T(8,128)S(1)}, f32[8,128]{1,0:T(8,128)S(1)}, f32[8,32]{1,0:T(8,128)S(1)}) custom-call(f32[8,512,128]{2,1,0:T(8,128)} %bitcast.8, f32[32,16,128]{2,1,0:T(8,128)} %scal.1, f32[32,16,128]{2,1,0:T(8,128)} %diag.1, f32[8,128]{1,0:T(8,128)} %bnd.1, s32[1,128]{1,0:T(1,128)} %bitcast.12, s32[1,128]{1,0:T(1,128)} %bitcast.13, ...), custom_call_target="tpu_custom_call" | custom-call | tf_op jit(solution)/shard_map/pallas_call | solution.py:487
  22.4 1.3 %shard_map.122 = (f32[8,512,128]{2,1,0:T(8,128)}, f32[8,128]{1,0:T(8,128)}, f32[8,32]{1,0:T(8,128)}) custom-call(f32[512,8,128]{2,1,0:T(8,128)S(1)} %get-tuple-element.9.field, f32[8,128]{1,0:T(8,128)S(1)} %get-tuple-element.10.rows, f32[8,32]{1,0:T(8,128)S(1)} %get-tuple-element.11.sums), custom_call_target="tpu_custom_call" | custom-call | tf_op jit(solution)/shard_map/pallas_call | solution.py:538

commit v6 on v5

--- a/solution.py
+++ b/solution.py
@@ -347,6 +347,9 @@
         l.start()
     l_bnd.wait()
     l_lab.wait()
+    l_scal.wait()
+    pltpu.make_async_copy(vbuf, vbuf, vol_sem).wait()
+    scale_pass(sbuf, vbuf, wbuf)
     pl.semaphore_wait(barrier, count)
 
     x_sends = [remote(bbuf, xbuf.at[pos], xs_sem.at[i], xr_sem, (*plane(a, b), group)) for i, (a, b) in enumerate(PLANE)]
@@ -359,9 +362,6 @@
     pl.when(own_group)(x_self.start)
     lbuf[gz] = labv[...]
 
-    l_scal.wait()
-    pltpu.make_async_copy(vbuf, vbuf, vol_sem).wait()
-    scale_pass(sbuf, vbuf, wbuf)
     for copy, to, come in halo:
         pl.when(to)(copy.start)
 

time: 23.9 us -> 23.9 us (level)
  no operation moved by 1% of the time
where the time goes in v6:
time: 23.9 us; the launch traced here: 23.8 us
  Pallas kernels  23.1 us (97%)
  between operations  0.64 us (3%)
    pallas_call x1, Pallas kernels, shards(): pl.pallas_call(kernel, out_shape=(pltpu.VMEM(field, F32), pltpu.VMEM((COL...  21.8 us
    pallas_call x1, Pallas kernels, shards(): pl.pallas_call(deliver, out_shape=(pltpu.HBM((COLS, nodes, CZ), F32), plt...  1.34 us

profile of v6, /device:TPU:0, one launch (start us, length us, event | category | flops | bytes accessed | tf_op | source)
XLA Modules:
  0.0 23.8 jit_solution(11724626063574940860)
XLA Ops:
  0.6 21.8 %shard_map.121 = (f32[512,8,128]{2,1,0:T(8,128)S(1)}, f32[8,128]{1,0:T(8,128)S(1)}, f32[8,32]{1,0:T(8,128)S(1)}) custom-call(f32[8,512,128]{2,1,0:T(8,128)} %bitcast.8, f32[32,16,128]{2,1,0:T(8,128)} %scal.1, f32[32,16,128]{2,1,0:T(8,128)} %diag.1, f32[8,128]{1,0:T(8,128)} %bnd.1, s32[1,128]{1,0:T(1,128)} %bitcast.12, s32[1,128]{1,0:T(1,128)} %bitcast.13, ...), custom_call_target="tpu_custom_call" | custom-call | tf_op jit(solution)/shard_map/pallas_call | solution.py:487
  22.4 1.3 %shard_map.122 = (f32[8,512,128]{2,1,0:T(8,128)}, f32[8,128]{1,0:T(8,128)}, f32[8,32]{1,0:T(8,128)}) custom-call(f32[512,8,128]{2,1,0:T(8,128)S(1)} %get-tuple-element.9.field, f32[8,128]{1,0:T(8,128)S(1)} %get-tuple-element.10.rows, f32[8,32]{1,0:T(8,128)S(1)} %get-tuple-element.11.sums), custom_call_target="tpu_custom_call" | custom-call | tf_op jit(solution)/shard_map/pallas_call | solution.py:538
